TPU v7x, 128 devices: a whole 4x4x4 slice. The times are simulated.
128 devices in a mesh: item: 8 (over x_lo, z), user: 16 (over x_hi, y, core).
Axes of the slice: x: 4 (x_hi: 2, x_lo: 2; x = x_hi * 2 + x_lo), y: 4, z: 4, core: 2. Of those that a mesh axis runs over, the one named last changes fastest.
Arguments:
- history: bfloat16 [128, 1024, 512], P(('item', 'user')), may hold values from -6 to 6
- hist_len: int32 [128], P(('item', 'user')), may hold values from 256 to 1024, as said below
- cand_ids: int32 [128, 128], P(('item', 'user')), may hold values from 0 to 383, as said below
- cand_lists: int32 [128, 4], P(('item', 'user')), may hold values from 0 to 15, as said below
- item_table: bfloat16 [6144, 512], P('user', 'item'), may hold values from -6 to 6
- w_in: bfloat16 [512, 2048], replicated, may hold values from -0.25 to 0.25
- w_out: bfloat16 [512, 512], replicated, may hold values from -0.25 to 0.25
- grad_cand: bfloat16 [128, 128, 512], P(('item', 'user')), may hold values from -6 to 6
Outputs:
- hist_out: bfloat16 [128, 1024, 512], P(('item', 'user'))
- cand_out: bfloat16 [128, 128, 512], P(('item', 'user'))
- table_grad: float32 [6144, 512], P('user', 'item')
Inputs may be any that keep to these rules, and one draw needn't show every extreme that they name: `hist_len`: some user has exactly 1024 events; positions at or past a user's length are padding. `cand_ids`: the 128 ids of one user are different. `cand_lists`: the 4 entries of user g are different and none equals g mod 16.
All inputs are finite; a program needn't handle non-finite values.
Results may differ from a plain program's by a relative error of at most 0.013.
Values may be sent and summed in bfloat16 or wider, within the bound.
A program may use at most 64 MiB of HBM per device.

v0:
```python
import jax
import jax.numpy as jnp
from jax import lax
from jax.sharding import PartitionSpec as P

H = 8
NORM_EPS = 1e-05


def from_behind(block, axis, distance):
    devices = range(lax.axis_size(axis))
    route = [((i - distance) % len(devices), i) for i in devices]
    return lax.ppermute(block, axis, route)


def silu_slope(pre_act):
    sigmoid = jax.nn.sigmoid(pre_act)
    return sigmoid * (1.0 + pre_act * (1.0 - sigmoid))


def normalize(rows_in):
    centred = rows_in - jnp.mean(rows_in, axis=-1, keepdims=True)
    inv_dev = lax.rsqrt(jnp.mean(centred * centred, axis=-1, keepdims=True) + NORM_EPS)
    return (centred * inv_dev, inv_dev)


def history_layer(events, length, projected, w_out):
    event_rows = events.shape[0]
    model_width = events.shape[1]
    head_size = model_width // H
    att_scale = head_size ** (-0.5)
    block_rows = min(512, event_rows)
    u_part = projected[:, :model_width]
    heads_v = projected[:, model_width : 2 * model_width].reshape(event_rows, H, head_size)
    heads_q = projected[:, 2 * model_width : 3 * model_width].reshape(event_rows, H, head_size)
    heads_k = projected[:, 3 * model_width :].reshape(event_rows, H, head_size)
    block_total = (length + block_rows - 1) // block_rows

    def query_block(q_index, result):
        q_start = q_index * block_rows
        q_tile = lax.dynamic_slice_in_dim(heads_q, q_start, block_rows, 0)
        q_pos = q_start + jnp.arange(block_rows)

        def key_block(k_index, running):
            k_start = k_index * block_rows
            k_tile = lax.dynamic_slice_in_dim(heads_k, k_start, block_rows, 0)
            v_tile = lax.dynamic_slice_in_dim(heads_v, k_start, block_rows, 0)
            k_pos = k_start + jnp.arange(block_rows)
            scores = (
                jnp.einsum("qhd,khd->hqk", q_tile, k_tile, preferred_element_type=jnp.float32)
                * att_scale
            )
            allowed = (k_pos[None, :] <= q_pos[:, None]) & (k_pos[None, :] < length)
            weights = jnp.where(allowed[None], jax.nn.silu(scores), 0.0).astype(jnp.bfloat16)
            return running + jnp.einsum(
                "hqk,khd->qhd", weights, v_tile, preferred_element_type=jnp.float32
            )

        attended = lax.fori_loop(
            0, q_index + 1, key_block, jnp.zeros((block_rows, H, head_size), jnp.float32)
        )
        normed = normalize(attended.reshape(block_rows, model_width))[0]
        u_tile = lax.dynamic_slice_in_dim(u_part, q_start, block_rows, 0)
        mixed_rows = (normed * u_tile.astype(jnp.float32)).astype(jnp.bfloat16)
        x_tile = lax.dynamic_slice_in_dim(events, q_start, block_rows, 0)
        layer_out = jnp.dot(mixed_rows, w_out, preferred_element_type=jnp.float32) + x_tile.astype(
            jnp.float32
        )
        layer_out = jnp.where((q_pos < length)[:, None], layer_out, 0.0).astype(jnp.bfloat16)
        return lax.dynamic_update_slice_in_dim(result, layer_out, q_start, 0)

    return lax.fori_loop(0, block_total, query_block, jnp.zeros_like(events))


def candidate_pass(
    cand_q, cand_u, cand_emb, keys_k, keys_v, valid_keys, skip_rows, w_out, grad_rows
):
    cand_rows = cand_q.shape[0]
    model_width = cand_q.shape[1]
    head_size = model_width // H
    att_scale = head_size ** (-0.5)
    heads_q = cand_q.reshape(cand_rows, H, head_size)
    heads_k = keys_k.reshape(-1, H, head_size)
    heads_v = keys_v.reshape(-1, H, head_size)
    scores = (
        jnp.einsum("qhd,khd->hqk", heads_q, heads_k, preferred_element_type=jnp.float32) * att_scale
    )
    weights = jnp.where(valid_keys[None, None, :], jax.nn.silu(scores), 0.0).astype(jnp.bfloat16)
    attended = jnp.einsum(
        "hqk,khd->qhd", weights, heads_v, preferred_element_type=jnp.float32
    ).reshape(cand_rows, model_width)
    normed, inv_dev = normalize(attended)
    u_rows = cand_u.astype(jnp.float32)
    mixed_rows = (normed * u_rows).astype(jnp.bfloat16)
    layer_out = (
        jnp.dot(mixed_rows, w_out, preferred_element_type=jnp.float32)
        + cand_emb.astype(jnp.float32)
    ).astype(jnp.bfloat16)
    grad_mixed = jnp.einsum("rd,ed->re", grad_rows, w_out, preferred_element_type=jnp.float32)
    grad_u = grad_mixed * normed
    grad_normed = grad_mixed * u_rows
    grad_att = inv_dev * (
        grad_normed
        - jnp.mean(grad_normed, axis=-1, keepdims=True)
        - normed * jnp.mean(grad_normed * normed, axis=-1, keepdims=True)
    )
    grad_att = grad_att.astype(jnp.bfloat16).reshape(cand_rows, H, head_size)
    grad_weights = jnp.einsum("qhd,khd->hqk", grad_att, heads_v, preferred_element_type=jnp.float32)
    grad_scores = (
        jnp.where(valid_keys[None, None, :], grad_weights * silu_slope(scores), 0.0) * att_scale
    ).astype(jnp.bfloat16)
    grad_q = jnp.einsum(
        "hqk,khd->qhd", grad_scores, heads_k, preferred_element_type=jnp.float32
    ).reshape(cand_rows, model_width)
    grad_k = jnp.einsum(
        "hqk,qhd->khd", grad_scores[:, :, skip_rows:], heads_q, preferred_element_type=jnp.float32
    ).reshape(-1, model_width)
    grad_v = jnp.einsum(
        "hqk,qhd->khd", weights[:, :, skip_rows:], grad_att, preferred_element_type=jnp.float32
    ).reshape(-1, model_width)
    return (layer_out, grad_u, grad_q, grad_k, grad_v)


def local(history, hist_len, cand_ids, cand_lists, item_table, w_in, w_out, grad_cand):
    events = history[0]
    length = hist_len[0]
    own_ids = cand_ids[0]
    my_lists = cand_lists[0]
    grad_rows = grad_cand[0]
    event_rows = events.shape[0]
    model_width = events.shape[1]
    cand_count = own_ids.shape[0]
    slot_count = my_lists.shape[0]
    part_rows = item_table.shape[0]
    cycle_size = lax.axis_size("user")
    cycle_pos = lax.axis_index("user")
    catalogue = jnp.arange(part_rows, dtype=jnp.int32)
    own_hot = (own_ids[:, None] == catalogue[None, :]).astype(jnp.bfloat16)
    cand_emb = jnp.dot(
        own_hot,
        lax.all_gather(item_table, "item", axis=1, tiled=True),
        preferred_element_type=jnp.float32,
    ).astype(jnp.bfloat16)
    projected = jax.nn.silu(jnp.dot(events, w_in, preferred_element_type=jnp.float32)).astype(
        jnp.bfloat16
    )
    cand_pre = jnp.dot(cand_emb, w_in, preferred_element_type=jnp.float32)
    cand_proj = jax.nn.silu(cand_pre).astype(jnp.bfloat16)
    cand_u = cand_proj[:, :model_width]
    cand_v = cand_proj[:, model_width : 2 * model_width]
    cand_q = cand_proj[:, 2 * model_width : 3 * model_width]
    cand_k = cand_proj[:, 3 * model_width :]
    block_kv = jnp.concatenate([cand_k, cand_v], 1)
    held_slots = jnp.zeros((slot_count, cand_count, 2 * model_width), jnp.bfloat16)

    def store_block(slots_now, moving, source):
        return jnp.where((my_lists == source)[:, None, None], moving[None], slots_now)

    def forward_turn(turn_no, carried):
        moving, slots_now = carried
        moving = from_behind(moving, "user", 1)
        return (moving, store_block(slots_now, moving, (cycle_pos - turn_no) % cycle_size))

    held_slots = lax.fori_loop(1, cycle_size, forward_turn, (block_kv, held_slots))[1]
    hist_out = history_layer(events, length, projected, w_out)
    slot_k = held_slots[:, :, :model_width].reshape(slot_count * cand_count, model_width)
    slot_v = held_slots[:, :, model_width:].reshape(slot_count * cand_count, model_width)
    keys_k = jnp.concatenate([projected[:, 3 * model_width :], cand_k, slot_k], 0)
    keys_v = jnp.concatenate([projected[:, model_width : 2 * model_width], cand_v, slot_v], 0)
    valid_keys = jnp.concatenate(
        [jnp.arange(event_rows) < length, jnp.ones(((1 + slot_count) * cand_count,), dtype=bool)], 0
    )
    cand_out, grad_u, grad_q, grad_k, grad_v = candidate_pass(
        cand_q, cand_u, cand_emb, keys_k, keys_v, valid_keys, event_rows, w_out, grad_rows
    )
    grad_own = jnp.concatenate([grad_k[:cand_count], grad_v[:cand_count]], 1)
    grad_slots = jnp.concatenate(
        [
            grad_k[cand_count:].reshape(slot_count, cand_count, model_width),
            grad_v[cand_count:].reshape(slot_count, cand_count, model_width),
        ],
        2,
    )

    def slot_terms(owner):
        matched = my_lists == owner % cycle_size
        return jnp.sum(jnp.where(matched[:, None, None], grad_slots, 0.0), 0)

    def give_back(turn_no, running):
        running = from_behind(running.astype(jnp.bfloat16), "user", 1).astype(running.dtype)
        return running + slot_terms(cycle_pos - turn_no)

    grad_home = lax.fori_loop(1, cycle_size + 1, give_back, grad_own)
    grad_proj = jnp.concatenate(
        [grad_u, grad_home[:, model_width:], grad_q, grad_home[:, :model_width]], 1
    )
    grad_pre = (grad_proj * silu_slope(cand_pre)).astype(jnp.bfloat16)
    grad_emb = jnp.einsum(
        "rf,df->rd", grad_pre, w_in, preferred_element_type=jnp.float32
    ) + grad_rows.astype(jnp.float32)
    table_terms = jnp.einsum(
        "cv,cd->vd", own_hot.astype(jnp.float32), grad_emb, precision=lax.Precision.HIGHEST
    )
    table_grad = lax.psum_scatter(
        table_terms.astype(jnp.bfloat16), "item", scatter_dimension=1, tiled=True
    ).astype(jnp.float32)
    return (hist_out[None], cand_out[None], table_grad)


def solution(mesh):
    in_specs = (
        P(("item", "user"), None, None),
        P(("item", "user")),
        P(("item", "user"), None),
        P(("item", "user"), None),
        P("user", "item"),
        P(),
        P(),
        P(("item", "user"), None, None),
    )
    out_specs = (
        P(("item", "user"), None, None),
        P(("item", "user"), None, None),
        P("user", "item"),
    )
    return jax.shard_map(local, mesh=mesh, in_specs=in_specs, out_specs=out_specs, check_vma=False)
```

profile of v0, /device:TPU:0, one launch (start us, length us, event | category | flops | bytes accessed | tf_op | source)
XLA Modules:
  0.0 472.5 jit_solution(8002575875772738989)
XLA Ops:
  7.2 30.4 %all_gather.3 = bf16[384,512]{0,1:T(8,128)(2,1)S(1)} all-gather(bf16[384,64]{0,1:T(8,128)(2,1)} %param.20), channel_id=1, replica_groups=mesh['item'=8,'user'=16] {'item'}, dimensions={1}, use_global_device_ids=true | all-gather | bytes 442368 | tf_op jit(solution)/shard_map/all_gather | solution.py:141
  43.8 4.2 multiply_convert_fusion
  48.0 2.1 fusion.61
  50.2 2.3 copy.34
  52.5 2.3 copy.35
  55.5 161.5 %while.57 = (s32[]{:T(128)}, bf16[128,1024]{1,0:T(8,128)(2,1)}, bf16[4,128,1024]{2,1,0:T(8,128)(2,1)S(1)}, s32[]{:T(128)}, s32[4]{0:T(128)S(1)}, /*index=5*/s32[]{:T(128)}, s32[]{:T(128)}, s32[]{:T(128)}, s32[]{:T(128)}) while((s32[]{:T(128)}, bf16[128,1024]{1,0:T(8,128)(2,1)}, bf16[4,128,1024]{2,1,0:T(8,128)(2,1)S(1)}, s32[]{:T(128)}, ...), condition=%wide.region_7.8_spmd.clone, body=%wide.region_6.7_spmd.clone.sunk | while | flops 1048595 | bytes 3932460 | solution.py:164
  55.5 9.6 %collective-permute-done.1 = bf16[128,1024]{1,0:T(8,128)(2,1)S(1)} collective-permute-done((bf16[128,1024]{1,0:T(8,128)(2,1)}, bf16[128,1024]{1,0:T(8,128)(2,1)S(1)}, u32[]{:S(2)}, u32[]{:S(2)}) %collective-permute-start.1) | collective-permute-done | bytes 262176 | tf_op jit(solution)/shard_map/while/body/eval_jaxpr/ppermute | solution.py:13
  66.4 9.6 %collective-permute-done.1 = bf16[128,1024]{1,0:T(8,128)(2,1)S(1)} collective-permute-done((bf16[128,1024]{1,0:T(8,128)(2,1)}, bf16[128,1024]{1,0:T(8,128)(2,1)S(1)}, u32[]{:S(2)}, u32[]{:S(2)}) %collective-permute-start.1) | collective-permute-done | bytes 262176 | tf_op jit(solution)/shard_map/while/body/eval_jaxpr/ppermute | solution.py:13
  77.1 9.6 %collective-permute-done.1 = bf16[128,1024]{1,0:T(8,128)(2,1)S(1)} collective-permute-done((bf16[128,1024]{1,0:T(8,128)(2,1)}, bf16[128,1024]{1,0:T(8,128)(2,1)S(1)}, u32[]{:S(2)}, u32[]{:S(2)}) %collective-permute-start.1) | collective-permute-done | bytes 262176 | tf_op jit(solution)/shard_map/while/body/eval_jaxpr/ppermute | solution.py:13
  87.9 9.6 %collective-permute-done.1 = bf16[128,1024]{1,0:T(8,128)(2,1)S(1)} collective-permute-done((bf16[128,1024]{1,0:T(8,128)(2,1)}, bf16[128,1024]{1,0:T(8,128)(2,1)S(1)}, u32[]{:S(2)}, u32[]{:S(2)}) %collective-permute-start.1) | collective-permute-done | bytes 262176 | tf_op jit(solution)/shard_map/while/body/eval_jaxpr/ppermute | solution.py:13
  98.7 9.6 %collective-permute-done.1 = bf16[128,1024]{1,0:T(8,128)(2,1)S(1)} collective-permute-done((bf16[128,1024]{1,0:T(8,128)(2,1)}, bf16[128,1024]{1,0:T(8,128)(2,1)S(1)}, u32[]{:S(2)}, u32[]{:S(2)}) %collective-permute-start.1) | collective-permute-done | bytes 262176 | tf_op jit(solution)/shard_map/while/body/eval_jaxpr/ppermute | solution.py:13
  109.5 9.6 %collective-permute-done.1 = bf16[128,1024]{1,0:T(8,128)(2,1)S(1)} collective-permute-done((bf16[128,1024]{1,0:T(8,128)(2,1)}, bf16[128,1024]{1,0:T(8,128)(2,1)S(1)}, u32[]{:S(2)}, u32[]{:S(2)}) %collective-permute-start.1) | collective-permute-done | bytes 262176 | tf_op jit(solution)/shard_map/while/body/eval_jaxpr/ppermute | solution.py:13
  120.2 9.6 %collective-permute-done.1 = bf16[128,1024]{1,0:T(8,128)(2,1)S(1)} collective-permute-done((bf16[128,1024]{1,0:T(8,128)(2,1)}, bf16[128,1024]{1,0:T(8,128)(2,1)S(1)}, u32[]{:S(2)}, u32[]{:S(2)}) %collective-permute-start.1) | collective-permute-done | bytes 262176 | tf_op jit(solution)/shard_map/while/body/eval_jaxpr/ppermute | solution.py:13
  131.0 9.6 %collective-permute-done.1 = bf16[128,1024]{1,0:T(8,128)(2,1)S(1)} collective-permute-done((bf16[128,1024]{1,0:T(8,128)(2,1)}, bf16[128,1024]{1,0:T(8,128)(2,1)S(1)}, u32[]{:S(2)}, u32[]{:S(2)}) %collective-permute-start.1) | collective-permute-done | bytes 262176 | tf_op jit(solution)/shard_map/while/body/eval_jaxpr/ppermute | solution.py:13
  141.8 9.6 %collective-permute-done.1 = bf16[128,1024]{1,0:T(8,128)(2,1)S(1)} collective-permute-done((bf16[128,1024]{1,0:T(8,128)(2,1)}, bf16[128,1024]{1,0:T(8,128)(2,1)S(1)}, u32[]{:S(2)}, u32[]{:S(2)}) %collective-permute-start.1) | collective-permute-done | bytes 262176 | tf_op jit(solution)/shard_map/while/body/eval_jaxpr/ppermute | solution.py:13
  152.5 9.6 %collective-permute-done.1 = bf16[128,1024]{1,0:T(8,128)(2,1)S(1)} collective-permute-done((bf16[128,1024]{1,0:T(8,128)(2,1)}, bf16[128,1024]{1,0:T(8,128)(2,1)S(1)}, u32[]{:S(2)}, u32[]{:S(2)}) %collective-permute-start.1) | collective-permute-done | bytes 262176 | tf_op jit(solution)/shard_map/while/body/eval_jaxpr/ppermute | solution.py:13
  163.3 9.6 %collective-permute-done.1 = bf16[128,1024]{1,0:T(8,128)(2,1)S(1)} collective-permute-done((bf16[128,1024]{1,0:T(8,128)(2,1)}, bf16[128,1024]{1,0:T(8,128)(2,1)S(1)}, u32[]{:S(2)}, u32[]{:S(2)}) %collective-permute-start.1) | collective-permute-done | bytes 262176 | tf_op jit(solution)/shard_map/while/body/eval_jaxpr/ppermute | solution.py:13
  174.1 9.6 %collective-permute-done.1 = bf16[128,1024]{1,0:T(8,128)(2,1)S(1)} collective-permute-done((bf16[128,1024]{1,0:T(8,128)(2,1)}, bf16[128,1024]{1,0:T(8,128)(2,1)S(1)}, u32[]{:S(2)}, u32[]{:S(2)}) %collective-permute-start.1) | collective-permute-done | bytes 262176 | tf_op jit(solution)/shard_map/while/body/eval_jaxpr/ppermute | solution.py:13
  184.9 9.6 %collective-permute-done.1 = bf16[128,1024]{1,0:T(8,128)(2,1)S(1)} collective-permute-done((bf16[128,1024]{1,0:T(8,128)(2,1)}, bf16[128,1024]{1,0:T(8,128)(2,1)S(1)}, u32[]{:S(2)}, u32[]{:S(2)}) %collective-permute-start.1) | collective-permute-done | bytes 262176 | tf_op jit(solution)/shard_map/while/body/eval_jaxpr/ppermute | solution.py:13
  195.6 9.6 %collective-permute-done.1 = bf16[128,1024]{1,0:T(8,128)(2,1)S(1)} collective-permute-done((bf16[128,1024]{1,0:T(8,128)(2,1)}, bf16[128,1024]{1,0:T(8,128)(2,1)S(1)}, u32[]{:S(2)}, u32[]{:S(2)}) %collective-permute-start.1) | collective-permute-done | bytes 262176 | tf_op jit(solution)/shard_map/while/body/eval_jaxpr/ppermute | solution.py:13
  206.4 9.6 %collective-permute-done.1 = bf16[128,1024]{1,0:T(8,128)(2,1)S(1)} collective-permute-done((bf16[128,1024]{1,0:T(8,128)(2,1)}, bf16[128,1024]{1,0:T(8,128)(2,1)S(1)}, u32[]{:S(2)}, u32[]{:S(2)}) %collective-permute-start.1) | collective-permute-done | bytes 262176 | tf_op jit(solution)/shard_map/while/body/eval_jaxpr/ppermute | solution.py:13
  222.3 6.4 %select_convert_fusion = (bf16[8,128,1664]{2,1,0:T(8,128)(2,1)S(1)}, f32[8,128,1664]{2,1,0:T(8,128)}) fusion(pred[1664]{0:T(1024)(128)(4,1)S(1)} %concatenate.35, bf16[128,8,64]{0,2,1:T(8,128)(2,1)S(1)} %bitcast.120, bf16[512,8,64]{0,2,1:T(8,128)(2,1)S(1)} %concatenate.37, bf16[128,8,64]{0,2,1:T(8,128)(2,1)S(1)} %bitcast.125, bf16[1024,8,64]{0,2,1:T(8,128)(2,1)} %bitcast.114), kind=kOutput, calls=%fused_computation.43 | convolution fusion | flops 235143168 | bytes 12060288 | tf_op jit(solution)/shard_map/qhd,khd->hqk/dot_general | solution.py:86
  228.8 2.1 fusion.65
  237.8 6.2 %multiply_convert_fusion.1 = bf16[8,128,1664]{2,1,0:T(8,128)(2,1)S(1)} fusion(f32[8,128,1664]{2,1,0:T(8,128)} %get-tuple-element.502, bf16[128,8,64]{0,2,1:T(8,128)(2,1)S(1)} %bitcast.123, pred[1664]{0:T(1024)(128)(4,1)S(1)} %concatenate.35, bf16[512,8,64]{0,2,1:T(8,128)(2,1)} %concatenate.33, bf16[128,8,64]{0,2,1:T(8,128)(2,1)} %bitcast.127, ...), kind=kOutput, calls=%fused_computation.42 | convolution fusion | flops 243662848 | bytes 12060288 | tf_op jit(solution)/shard_map/qhd,khd->hqk/dot_general | solution.py:108
  246.3 2.1 fusion.36
  252.4 2.6 copy.47
  258.8 3.1 pad_maximum_fusion
  261.9 153.9 %while.56 = (s32[]{:T(128)}, f32[128,1024]{1,0:T(8,128)S(1)}, s32[]{:T(128)}, s32[4]{0:T(128)S(1)}, f32[4,128,1024]{2,1,0:T(8,128)}, /*index=5*/s32[]{:T(128)}, s32[]{:T(128)}, s32[]{:T(128)}, s32[]{:T(128)}) while((s32[]{:T(128)}, f32[128,1024]{1,0:T(8,128)S(1)}, s32[]{:T(128)}, s32[4]{0:T(128)S(1)}, f32[4,128,1024]{2,1,0:T(8,128)}, ...), condition=%wide.region_14.15_spmd, body=%wide.region_12.14_spmd.sunk | while | flops 1310738 | bytes 5767450 | solution.py:193
  262.1 1.9 select_reduce_fusion.2
  264.0 7.4 %collective-permute-done = bf16[128,1024]{1,0:T(8,128)(2,1)S(1)} collective-permute-done((bf16[128,1024]{1,0:T(8,128)(2,1)S(1)}, bf16[128,1024]{1,0:T(8,128)(2,1)S(1)}, u32[]{:S(2)}, u32[]{:S(2)}) %collective-permute-start) | collective-permute-done | bytes 262176 | tf_op jit(solution)/shard_map/while/body/eval_jaxpr/ppermute | solution.py:13
  271.7 1.9 select_reduce_fusion.2
  273.6 7.4 %collective-permute-done = bf16[128,1024]{1,0:T(8,128)(2,1)S(1)} collective-permute-done((bf16[128,1024]{1,0:T(8,128)(2,1)S(1)}, bf16[128,1024]{1,0:T(8,128)(2,1)S(1)}, u32[]{:S(2)}, u32[]{:S(2)}) %collective-permute-start) | collective-permute-done | bytes 262176 | tf_op jit(solution)/shard_map/while/body/eval_jaxpr/ppermute | solution.py:13
  283.2 7.4 %collective-permute-done = bf16[128,1024]{1,0:T(8,128)(2,1)S(1)} collective-permute-done((bf16[128,1024]{1,0:T(8,128)(2,1)S(1)}, bf16[128,1024]{1,0:T(8,128)(2,1)S(1)}, u32[]{:S(2)}, u32[]{:S(2)}) %collective-permute-start) | collective-permute-done | bytes 262176 | tf_op jit(solution)/shard_map/while/body/eval_jaxpr/ppermute | solution.py:13
  290.9 1.9 select_reduce_fusion.2
  292.8 7.4 %collective-permute-done = bf16[128,1024]{1,0:T(8,128)(2,1)S(1)} collective-permute-done((bf16[128,1024]{1,0:T(8,128)(2,1)S(1)}, bf16[128,1024]{1,0:T(8,128)(2,1)S(1)}, u32[]{:S(2)}, u32[]{:S(2)}) %collective-permute-start) | collective-permute-done | bytes 262176 | tf_op jit(solution)/shard_map/while/body/eval_jaxpr/ppermute | solution.py:13
  302.5 7.4 %collective-permute-done = bf16[128,1024]{1,0:T(8,128)(2,1)S(1)} collective-permute-done((bf16[128,1024]{1,0:T(8,128)(2,1)S(1)}, bf16[128,1024]{1,0:T(8,128)(2,1)S(1)}, u32[]{:S(2)}, u32[]{:S(2)}) %collective-permute-start) | collective-permute-done | bytes 262176 | tf_op jit(solution)/shard_map/while/body/eval_jaxpr/ppermute | solution.py:13
  312.1 7.4 %collective-permute-done = bf16[128,1024]{1,0:T(8,128)(2,1)S(1)} collective-permute-done((bf16[128,1024]{1,0:T(8,128)(2,1)S(1)}, bf16[128,1024]{1,0:T(8,128)(2,1)S(1)}, u32[]{:S(2)}, u32[]{:S(2)}) %collective-permute-start) | collective-permute-done | bytes 262176 | tf_op jit(solution)/shard_map/while/body/eval_jaxpr/ppermute | solution.py:13
  321.7 7.4 %collective-permute-done = bf16[128,1024]{1,0:T(8,128)(2,1)S(1)} collective-permute-done((bf16[128,1024]{1,0:T(8,128)(2,1)S(1)}, bf16[128,1024]{1,0:T(8,128)(2,1)S(1)}, u32[]{:S(2)}, u32[]{:S(2)}) %collective-permute-start) | collective-permute-done | bytes 262176 | tf_op jit(solution)/shard_map/while/body/eval_jaxpr/ppermute | solution.py:13
  329.3 1.9 select_reduce_fusion.2
  331.3 7.4 %collective-permute-done = bf16[128,1024]{1,0:T(8,128)(2,1)S(1)} collective-permute-done((bf16[128,1024]{1,0:T(8,128)(2,1)S(1)}, bf16[128,1024]{1,0:T(8,128)(2,1)S(1)}, u32[]{:S(2)}, u32[]{:S(2)}) %collective-permute-start) | collective-permute-done | bytes 262176 | tf_op jit(solution)/shard_map/while/body/eval_jaxpr/ppermute | solution.py:13
  340.9 7.4 %collective-permute-done = bf16[128,1024]{1,0:T(8,128)(2,1)S(1)} collective-permute-done((bf16[128,1024]{1,0:T(8,128)(2,1)S(1)}, bf16[128,1024]{1,0:T(8,128)(2,1)S(1)}, u32[]{:S(2)}, u32[]{:S(2)}) %collective-permute-start) | collective-permute-done | bytes 262176 | tf_op jit(solution)/shard_map/while/body/eval_jaxpr/ppermute | solution.py:13
  350.5 7.4 %collective-permute-done = bf16[128,1024]{1,0:T(8,128)(2,1)S(1)} collective-permute-done((bf16[128,1024]{1,0:T(8,128)(2,1)S(1)}, bf16[128,1024]{1,0:T(8,128)(2,1)S(1)}, u32[]{:S(2)}, u32[]{:S(2)}) %collective-permute-start) | collective-permute-done | bytes 262176 | tf_op jit(solution)/shard_map/while/body/eval_jaxpr/ppermute | solution.py:13
  358.2 1.9 select_reduce_fusion.2
  360.1 7.4 %collective-permute-done = bf16[128,1024]{1,0:T(8,128)(2,1)S(1)} collective-permute-done((bf16[128,1024]{1,0:T(8,128)(2,1)S(1)}, bf16[128,1024]{1,0:T(8,128)(2,1)S(1)}, u32[]{:S(2)}, u32[]{:S(2)}) %collective-permute-start) | collective-permute-done | bytes 262176 | tf_op jit(solution)/shard_map/while/body/eval_jaxpr/ppermute | solution.py:13
  367.8 1.9 select_reduce_fusion.2
  369.7 7.4 %collective-permute-done = bf16[128,1024]{1,0:T(8,128)(2,1)S(1)} collective-permute-done((bf16[128,1024]{1,0:T(8,128)(2,1)S(1)}, bf16[128,1024]{1,0:T(8,128)(2,1)S(1)}, u32[]{:S(2)}, u32[]{:S(2)}) %collective-permute-start) | collective-permute-done | bytes 262176 | tf_op jit(solution)/shard_map/while/body/eval_jaxpr/ppermute | solution.py:13
  379.3 7.4 %collective-permute-done = bf16[128,1024]{1,0:T(8,128)(2,1)S(1)} collective-permute-done((bf16[128,1024]{1,0:T(8,128)(2,1)S(1)}, bf16[128,1024]{1,0:T(8,128)(2,1)S(1)}, u32[]{:S(2)}, u32[]{:S(2)}) %collective-permute-start) | collective-permute-done | bytes 262176 | tf_op jit(solution)/shard_map/while/body/eval_jaxpr/ppermute | solution.py:13
  388.9 7.4 %collective-permute-done = bf16[128,1024]{1,0:T(8,128)(2,1)S(1)} collective-permute-done((bf16[128,1024]{1,0:T(8,128)(2,1)S(1)}, bf16[128,1024]{1,0:T(8,128)(2,1)S(1)}, u32[]{:S(2)}, u32[]{:S(2)}) %collective-permute-start) | collective-permute-done | bytes 262176 | tf_op jit(solution)/shard_map/while/body/eval_jaxpr/ppermute | solution.py:13
  396.6 1.9 select_reduce_fusion.2
  398.5 7.4 %collective-permute-done = bf16[128,1024]{1,0:T(8,128)(2,1)S(1)} collective-permute-done((bf16[128,1024]{1,0:T(8,128)(2,1)S(1)}, bf16[128,1024]{1,0:T(8,128)(2,1)S(1)}, u32[]{:S(2)}, u32[]{:S(2)}) %collective-permute-start) | collective-permute-done | bytes 262176 | tf_op jit(solution)/shard_map/while/body/eval_jaxpr/ppermute | solution.py:13
  406.2 1.9 select_reduce_fusion.2
  408.1 7.4 %collective-permute-done = bf16[128,1024]{1,0:T(8,128)(2,1)S(1)} collective-permute-done((bf16[128,1024]{1,0:T(8,128)(2,1)S(1)}, bf16[128,1024]{1,0:T(8,128)(2,1)S(1)}, u32[]{:S(2)}, u32[]{:S(2)}) %collective-permute-start) | collective-permute-done | bytes 262176 | tf_op jit(solution)/shard_map/while/body/eval_jaxpr/ppermute | solution.py:13
  417.5 2.5 convolution_add_fusion.1
  423.7 38.3 %while.55 = (s32[]{:T(128)}, bf16[1024,512]{1,0:T(8,128)(2,1)}, s32[]{:T(128)}, s32[]{:T(128)}, bf16[1024,8,64]{0,2,1:T(8,128)(2,1)}, /*index=5*/bf16[1024,8,64]...) while((s32[]{:T(128)}, bf16[1024,512]{1,0:T(8,128)(2,1)}, ...), condition=%wide.region_5.6_spmd, body=%wide.region_0.5_spmd.sunk | while | flops 824184320 | bytes 14710306 | solution.py:72
  425.8 5.6 %while.58 = (s32[]{:T(128)}, f32[512,8,64]{0,2,1:T(8,128)S(1)}, s32[]{:T(128)}, bf16[1024,8,64]{0,2,1:T(8,128)(2,1)}, s32[]{:T(128)}, /*index=5*/bf16[1024,8,64]...) while((s32[]{:T(128)}, f32[512,8,64]{0,2,1:T(8,128)S(1)}, ...), condition=%wide.region_2.2_spmd.clone, body=%wide.region_1.1_spmd.clone.sunk | while | flops 552339456 | bytes 4204731 | solution.py:59
  426.7 4.7 fusion.100
  433.3 2.0 copy.52
  437.6 2.5 fusion.95
  442.1 11.3 %while.58 = (s32[]{:T(128)}, f32[512,8,64]{0,2,1:T(8,128)S(1)}, s32[]{:T(128)}, bf16[1024,8,64]{0,2,1:T(8,128)(2,1)}, s32[]{:T(128)}, /*index=5*/bf16[1024,8,64]...) while((s32[]{:T(128)}, f32[512,8,64]{0,2,1:T(8,128)S(1)}, ...), condition=%wide.region_2.2_spmd.clone, body=%wide.region_1.1_spmd.clone.sunk | while | flops 552339456 | bytes 4204731 | solution.py:59
  443.0 4.7 fusion.100
  448.7 4.7 fusion.100
  455.3 2.0 copy.52
  459.5 2.5 fusion.95
  462.0 2.1 fusion.34
  (263 shorter events, 85.9 us)
Async XLA Ops:
  7.2 31.4 %copy-start = (bf16[512,2048]{1,0:T(8,128)(2,1)S(1)}, bf16[512,2048]{1,0:T(8,128)(2,1)}, u32[]{:S(2)}) copy-start(bf16[512,2048]{1,0:T(8,128)(2,1)} %param.21) | copy-start | bytes 6291460
  7.2 457.0 %reduce-scatter.2.cloned.1.call-start = ((), (), s32[]{:S(2)}) async-start(), calls=%async_computation.1 | async-start | bytes 442368 | tf_op jit(solution)/shard_map/reduce_scatter | solution.py:204
  38.6 2.3 copy-start.13
  40.0 0.8 copy-start.5
  50.2 5.4 %copy-start.28 = (s32[1,4]{1,0:T(1,128)S(1)}, s32[1,4]{1,0:T(1,128)}, u32[]{:S(2)}) copy-start(s32[1,4]{1,0:T(1,128)} %param.19) | copy-start | bytes 52
  55.5 9.6 %collective-permute-start.1 = (bf16[128,1024]{1,0:T(8,128)(2,1)}, bf16[128,1024]{1,0:T(8,128)(2,1)S(1)}, u32[]{:S(2)}, u32[]{:S(2)}) collective-permute-start(bf16[128,1024]{1,0:T(8,128)(2,1)} %get-tuple-element.808), channel_id=1, source_target_pairs={{15,0},{0,1},{1,2},{2,3},{3,4},{4,5},{5,6},{6,7},{7,8},{8,9},{9,10... | collective-permute-start | bytes 786440 | tf_op jit(solution)/shard_map/while/body/eval_jaxpr/ppermute | solution.py:13
  66.2 9.7 %collective-permute-start.1 = (bf16[128,1024]{1,0:T(8,128)(2,1)}, bf16[128,1024]{1,0:T(8,128)(2,1)S(1)}, u32[]{:S(2)}, u32[]{:S(2)}) collective-permute-start(bf16[128,1024]{1,0:T(8,128)(2,1)} %get-tuple-element.808), channel_id=1, source_target_pairs={{15,0},{0,1},{1,2},{2,3},{3,4},{4,5},{5,6},{6,7},{7,8},{8,9},{9,10... | collective-permute-start | bytes 786440 | tf_op jit(solution)/shard_map/while/body/eval_jaxpr/ppermute | solution.py:13
  77.0 9.7 %collective-permute-start.1 = (bf16[128,1024]{1,0:T(8,128)(2,1)}, bf16[128,1024]{1,0:T(8,128)(2,1)S(1)}, u32[]{:S(2)}, u32[]{:S(2)}) collective-permute-start(bf16[128,1024]{1,0:T(8,128)(2,1)} %get-tuple-element.808), channel_id=1, source_target_pairs={{15,0},{0,1},{1,2},{2,3},{3,4},{4,5},{5,6},{6,7},{7,8},{8,9},{9,10... | collective-permute-start | bytes 786440 | tf_op jit(solution)/shard_map/while/body/eval_jaxpr/ppermute | solution.py:13
  87.8 9.7 %collective-permute-start.1 = (bf16[128,1024]{1,0:T(8,128)(2,1)}, bf16[128,1024]{1,0:T(8,128)(2,1)S(1)}, u32[]{:S(2)}, u32[]{:S(2)}) collective-permute-start(bf16[128,1024]{1,0:T(8,128)(2,1)} %get-tuple-element.808), channel_id=1, source_target_pairs={{15,0},{0,1},{1,2},{2,3},{3,4},{4,5},{5,6},{6,7},{7,8},{8,9},{9,10... | collective-permute-start | bytes 786440 | tf_op jit(solution)/shard_map/while/body/eval_jaxpr/ppermute | solution.py:13
  98.6 9.7 %collective-permute-start.1 = (bf16[128,1024]{1,0:T(8,128)(2,1)}, bf16[128,1024]{1,0:T(8,128)(2,1)S(1)}, u32[]{:S(2)}, u32[]{:S(2)}) collective-permute-start(bf16[128,1024]{1,0:T(8,128)(2,1)} %get-tuple-element.808), channel_id=1, source_target_pairs={{15,0},{0,1},{1,2},{2,3},{3,4},{4,5},{5,6},{6,7},{7,8},{8,9},{9,10... | collective-permute-start | bytes 786440 | tf_op jit(solution)/shard_map/while/body/eval_jaxpr/ppermute | solution.py:13
  109.3 9.7 %collective-permute-start.1 = (bf16[128,1024]{1,0:T(8,128)(2,1)}, bf16[128,1024]{1,0:T(8,128)(2,1)S(1)}, u32[]{:S(2)}, u32[]{:S(2)}) collective-permute-start(bf16[128,1024]{1,0:T(8,128)(2,1)} %get-tuple-element.808), channel_id=1, source_target_pairs={{15,0},{0,1},{1,2},{2,3},{3,4},{4,5},{5,6},{6,7},{7,8},{8,9},{9,10... | collective-permute-start | bytes 786440 | tf_op jit(solution)/shard_map/while/body/eval_jaxpr/ppermute | solution.py:13
  120.1 9.7 %collective-permute-start.1 = (bf16[128,1024]{1,0:T(8,128)(2,1)}, bf16[128,1024]{1,0:T(8,128)(2,1)S(1)}, u32[]{:S(2)}, u32[]{:S(2)}) collective-permute-start(bf16[128,1024]{1,0:T(8,128)(2,1)} %get-tuple-element.808), channel_id=1, source_target_pairs={{15,0},{0,1},{1,2},{2,3},{3,4},{4,5},{5,6},{6,7},{7,8},{8,9},{9,10... | collective-permute-start | bytes 786440 | tf_op jit(solution)/shard_map/while/body/eval_jaxpr/ppermute | solution.py:13
  130.9 9.7 %collective-permute-start.1 = (bf16[128,1024]{1,0:T(8,128)(2,1)}, bf16[128,1024]{1,0:T(8,128)(2,1)S(1)}, u32[]{:S(2)}, u32[]{:S(2)}) collective-permute-start(bf16[128,1024]{1,0:T(8,128)(2,1)} %get-tuple-element.808), channel_id=1, source_target_pairs={{15,0},{0,1},{1,2},{2,3},{3,4},{4,5},{5,6},{6,7},{7,8},{8,9},{9,10... | collective-permute-start | bytes 786440 | tf_op jit(solution)/shard_map/while/body/eval_jaxpr/ppermute | solution.py:13
  141.7 9.7 %collective-permute-start.1 = (bf16[128,1024]{1,0:T(8,128)(2,1)}, bf16[128,1024]{1,0:T(8,128)(2,1)S(1)}, u32[]{:S(2)}, u32[]{:S(2)}) collective-permute-start(bf16[128,1024]{1,0:T(8,128)(2,1)} %get-tuple-element.808), channel_id=1, source_target_pairs={{15,0},{0,1},{1,2},{2,3},{3,4},{4,5},{5,6},{6,7},{7,8},{8,9},{9,10... | collective-permute-start | bytes 786440 | tf_op jit(solution)/shard_map/while/body/eval_jaxpr/ppermute | solution.py:13
  152.4 9.7 %collective-permute-start.1 = (bf16[128,1024]{1,0:T(8,128)(2,1)}, bf16[128,1024]{1,0:T(8,128)(2,1)S(1)}, u32[]{:S(2)}, u32[]{:S(2)}) collective-permute-start(bf16[128,1024]{1,0:T(8,128)(2,1)} %get-tuple-element.808), channel_id=1, source_target_pairs={{15,0},{0,1},{1,2},{2,3},{3,4},{4,5},{5,6},{6,7},{7,8},{8,9},{9,10... | collective-permute-start | bytes 786440 | tf_op jit(solution)/shard_map/while/body/eval_jaxpr/ppermute | solution.py:13
  163.2 9.7 %collective-permute-start.1 = (bf16[128,1024]{1,0:T(8,128)(2,1)}, bf16[128,1024]{1,0:T(8,128)(2,1)S(1)}, u32[]{:S(2)}, u32[]{:S(2)}) collective-permute-start(bf16[128,1024]{1,0:T(8,128)(2,1)} %get-tuple-element.808), channel_id=1, source_target_pairs={{15,0},{0,1},{1,2},{2,3},{3,4},{4,5},{5,6},{6,7},{7,8},{8,9},{9,10... | collective-permute-start | bytes 786440 | tf_op jit(solution)/shard_map/while/body/eval_jaxpr/ppermute | solution.py:13
  174.0 9.7 %collective-permute-start.1 = (bf16[128,1024]{1,0:T(8,128)(2,1)}, bf16[128,1024]{1,0:T(8,128)(2,1)S(1)}, u32[]{:S(2)}, u32[]{:S(2)}) collective-permute-start(bf16[128,1024]{1,0:T(8,128)(2,1)} %get-tuple-element.808), channel_id=1, source_target_pairs={{15,0},{0,1},{1,2},{2,3},{3,4},{4,5},{5,6},{6,7},{7,8},{8,9},{9,10... | collective-permute-start | bytes 786440 | tf_op jit(solution)/shard_map/while/body/eval_jaxpr/ppermute | solution.py:13
  184.7 9.7 %collective-permute-start.1 = (bf16[128,1024]{1,0:T(8,128)(2,1)}, bf16[128,1024]{1,0:T(8,128)(2,1)S(1)}, u32[]{:S(2)}, u32[]{:S(2)}) collective-permute-start(bf16[128,1024]{1,0:T(8,128)(2,1)} %get-tuple-element.808), channel_id=1, source_target_pairs={{15,0},{0,1},{1,2},{2,3},{3,4},{4,5},{5,6},{6,7},{7,8},{8,9},{9,10... | collective-permute-start | bytes 786440 | tf_op jit(solution)/shard_map/while/body/eval_jaxpr/ppermute | solution.py:13
  195.5 9.7 %collective-permute-start.1 = (bf16[128,1024]{1,0:T(8,128)(2,1)}, bf16[128,1024]{1,0:T(8,128)(2,1)S(1)}, u32[]{:S(2)}, u32[]{:S(2)}) collective-permute-start(bf16[128,1024]{1,0:T(8,128)(2,1)} %get-tuple-element.808), channel_id=1, source_target_pairs={{15,0},{0,1},{1,2},{2,3},{3,4},{4,5},{5,6},{6,7},{7,8},{8,9},{9,10... | collective-permute-start | bytes 786440 | tf_op jit(solution)/shard_map/while/body/eval_jaxpr/ppermute | solution.py:13
  206.3 9.7 %collective-permute-start.1 = (bf16[128,1024]{1,0:T(8,128)(2,1)}, bf16[128,1024]{1,0:T(8,128)(2,1)S(1)}, u32[]{:S(2)}, u32[]{:S(2)}) collective-permute-start(bf16[128,1024]{1,0:T(8,128)(2,1)} %get-tuple-element.808), channel_id=1, source_target_pairs={{15,0},{0,1},{1,2},{2,3},{3,4},{4,5},{5,6},{6,7},{7,8},{8,9},{9,10... | collective-permute-start | bytes 786440 | tf_op jit(solution)/shard_map/while/body/eval_jaxpr/ppermute | solution.py:13
  217.1 5.2 %copy-start.15 = (bf16[128,512]{0,1:T(8,128)(2,1)S(1)}, bf16[128,512]{0,1:T(8,128)(2,1)}, u32[]{:S(2)}) copy-start(bf16[128,512]{0,1:T(8,128)(2,1)} %copy.39) | copy-start | bytes 393220
  217.1 5.2 %copy-start.20 = (bf16[128,512]{0,1:T(8,128)(2,1)S(1)}, bf16[128,512]{0,1:T(8,128)(2,1)}, u32[]{:S(2)}) copy-start(bf16[128,512]{0,1:T(8,128)(2,1)} %copy.40) | copy-start | bytes 393220
  219.7 9.0 %copy-start.10 = (bf16[512,8,64]{0,2,1:T(8,128)(2,1)}, bf16[512,8,64]{0,2,1:T(8,128)(2,1)S(1)}, u32[]{:S(2)}) copy-start(bf16[512,8,64]{0,2,1:T(8,128)(2,1)S(1)} %concatenate.37) | copy-start | bytes 1572868
  222.3 6.4 %copy-start.7 = (bf16[1024,512]{0,1:T(8,128)(2,1)S(1)}, bf16[1024,512]{0,1:T(8,128)(2,1)}, u32[]{:S(2)}) copy-start(bf16[1024,512]{0,1:T(8,128)(2,1)} %copy.34) | copy-start | bytes 3145732
  222.3 6.4 %copy-start.12 = (bf16[512,8,64]{0,2,1:T(8,128)(2,1)S(1)}, bf16[512,8,64]{0,2,1:T(8,128)(2,1)}, u32[]{:S(2)}) copy-start(bf16[512,8,64]{0,2,1:T(8,128)(2,1)} %concatenate.33) | copy-start | bytes 1572868
  222.3 6.4 %copy-start.22 = (bf16[128,512]{0,1:T(8,128)(2,1)S(1)}, bf16[128,512]{0,1:T(8,128)(2,1)}, u32[]{:S(2)}) copy-start(bf16[128,512]{0,1:T(8,128)(2,1)} %copy.37) | copy-start | bytes 393220
  228.7 2.1 copy-start.17
  228.7 4.3 copy-start.4
  228.7 4.3 copy-start.6
  231.9 4.1 copy-start.2
  231.9 3.3 copy-start.23
  233.1 2.2 copy-start.25
  236.0 1.8 copy-start.16
  237.8 6.2 %copy-start.1 = (f32[640,8,64]{0,2,1:T(8,128)}, f32[640,8,64]{0,2,1:T(8,128)S(1)}, u32[]{:S(2)}) copy-start(f32[640,8,64]{0,2,1:T(8,128)S(1)} %convolution_bitcast_fusion) | copy-start | bytes 3932164
  244.0 2.3 copy-start.8
  244.0 2.3 copy-start.11
  244.0 2.3 copy-start.21
  246.3 2.1 slice-start
  246.3 4.7 slice-start.1
  252.4 5.5 %copy-start.9 = (f32[128,512]{1,0:T(8,128)S(1)}, f32[128,512]{1,0:T(8,128)}, u32[]{:S(2)}) copy-start(f32[128,512]{1,0:T(8,128)} %copy.45) | copy-start | bytes 786436
  261.9 154.8 %copy-start.18 = (f32[8,64,128]{2,1,0:T(8,128)S(1)}, f32[8,64,128]{2,1,0:T(8,128)}, u32[]{:S(2)}) copy-start(f32[8,64,128]{2,1,0:T(8,128)} %fusion.36) | copy-start | bytes 786436
  261.9 155.6 %copy-start.19 = (bf16[1,128,512]{2,1,0:T(8,128)(2,1)S(1)}, bf16[1,128,512]{2,1,0:T(8,128)(2,1)}, u32[]{:S(2)}) copy-start(bf16[1,128,512]{2,1,0:T(8,128)(2,1)} %param.23) | copy-start | bytes 393220
  262.0 9.5 %collective-permute-start = (bf16[128,1024]{1,0:T(8,128)(2,1)S(1)}, bf16[128,1024]{1,0:T(8,128)(2,1)S(1)}, u32[]{:S(2)}, u32[]{:S(2)}) collective-permute-start(bf16[128,1024]{1,0:T(8,128)(2,1)S(1)} %convert_element_type.146), channel_id=1, source_target_pairs={{15,0},{0,1},{1,2},{2,3},{3,4},{4,5},{5,6},{6,7},{7,8},{8,9},{9,10... | collective-permute-start | bytes 786440 | tf_op jit(solution)/shard_map/while/body/eval_jaxpr/ppermute | solution.py:13
  271.6 9.5 %collective-permute-start = (bf16[128,1024]{1,0:T(8,128)(2,1)S(1)}, bf16[128,1024]{1,0:T(8,128)(2,1)S(1)}, u32[]{:S(2)}, u32[]{:S(2)}) collective-permute-start(bf16[128,1024]{1,0:T(8,128)(2,1)S(1)} %convert_element_type.146), channel_id=1, source_target_pairs={{15,0},{0,1},{1,2},{2,3},{3,4},{4,5},{5,6},{6,7},{7,8},{8,9},{9,10... | collective-permute-start | bytes 786440 | tf_op jit(solution)/shard_map/while/body/eval_jaxpr/ppermute | solution.py:13
  281.2 9.5 %collective-permute-start = (bf16[128,1024]{1,0:T(8,128)(2,1)S(1)}, bf16[128,1024]{1,0:T(8,128)(2,1)S(1)}, u32[]{:S(2)}, u32[]{:S(2)}) collective-permute-start(bf16[128,1024]{1,0:T(8,128)(2,1)S(1)} %convert_element_type.146), channel_id=1, source_target_pairs={{15,0},{0,1},{1,2},{2,3},{3,4},{4,5},{5,6},{6,7},{7,8},{8,9},{9,10... | collective-permute-start | bytes 786440 | tf_op jit(solution)/shard_map/while/body/eval_jaxpr/ppermute | solution.py:13
  290.8 9.5 %collective-permute-start = (bf16[128,1024]{1,0:T(8,128)(2,1)S(1)}, bf16[128,1024]{1,0:T(8,128)(2,1)S(1)}, u32[]{:S(2)}, u32[]{:S(2)}) collective-permute-start(bf16[128,1024]{1,0:T(8,128)(2,1)S(1)} %convert_element_type.146), channel_id=1, source_target_pairs={{15,0},{0,1},{1,2},{2,3},{3,4},{4,5},{5,6},{6,7},{7,8},{8,9},{9,10... | collective-permute-start | bytes 786440 | tf_op jit(solution)/shard_map/while/body/eval_jaxpr/ppermute | solution.py:13
  300.4 9.5 %collective-permute-start = (bf16[128,1024]{1,0:T(8,128)(2,1)S(1)}, bf16[128,1024]{1,0:T(8,128)(2,1)S(1)}, u32[]{:S(2)}, u32[]{:S(2)}) collective-permute-start(bf16[128,1024]{1,0:T(8,128)(2,1)S(1)} %convert_element_type.146), channel_id=1, source_target_pairs={{15,0},{0,1},{1,2},{2,3},{3,4},{4,5},{5,6},{6,7},{7,8},{8,9},{9,10... | collective-permute-start | bytes 786440 | tf_op jit(solution)/shard_map/while/body/eval_jaxpr/ppermute | solution.py:13
  310.0 9.5 %collective-permute-start = (bf16[128,1024]{1,0:T(8,128)(2,1)S(1)}, bf16[128,1024]{1,0:T(8,128)(2,1)S(1)}, u32[]{:S(2)}, u32[]{:S(2)}) collective-permute-start(bf16[128,1024]{1,0:T(8,128)(2,1)S(1)} %convert_element_type.146), channel_id=1, source_target_pairs={{15,0},{0,1},{1,2},{2,3},{3,4},{4,5},{5,6},{6,7},{7,8},{8,9},{9,10... | collective-permute-start | bytes 786440 | tf_op jit(solution)/shard_map/while/body/eval_jaxpr/ppermute | solution.py:13
  319.6 9.5 %collective-permute-start = (bf16[128,1024]{1,0:T(8,128)(2,1)S(1)}, bf16[128,1024]{1,0:T(8,128)(2,1)S(1)}, u32[]{:S(2)}, u32[]{:S(2)}) collective-permute-start(bf16[128,1024]{1,0:T(8,128)(2,1)S(1)} %convert_element_type.146), channel_id=1, source_target_pairs={{15,0},{0,1},{1,2},{2,3},{3,4},{4,5},{5,6},{6,7},{7,8},{8,9},{9,10... | collective-permute-start | bytes 786440 | tf_op jit(solution)/shard_map/while/body/eval_jaxpr/ppermute | solution.py:13
  329.2 9.5 %collective-permute-start = (bf16[128,1024]{1,0:T(8,128)(2,1)S(1)}, bf16[128,1024]{1,0:T(8,128)(2,1)S(1)}, u32[]{:S(2)}, u32[]{:S(2)}) collective-permute-start(bf16[128,1024]{1,0:T(8,128)(2,1)S(1)} %convert_element_type.146), channel_id=1, source_target_pairs={{15,0},{0,1},{1,2},{2,3},{3,4},{4,5},{5,6},{6,7},{7,8},{8,9},{9,10... | collective-permute-start | bytes 786440 | tf_op jit(solution)/shard_map/while/body/eval_jaxpr/ppermute | solution.py:13
  338.8 9.5 %collective-permute-start = (bf16[128,1024]{1,0:T(8,128)(2,1)S(1)}, bf16[128,1024]{1,0:T(8,128)(2,1)S(1)}, u32[]{:S(2)}, u32[]{:S(2)}) collective-permute-start(bf16[128,1024]{1,0:T(8,128)(2,1)S(1)} %convert_element_type.146), channel_id=1, source_target_pairs={{15,0},{0,1},{1,2},{2,3},{3,4},{4,5},{5,6},{6,7},{7,8},{8,9},{9,10... | collective-permute-start | bytes 786440 | tf_op jit(solution)/shard_map/while/body/eval_jaxpr/ppermute | solution.py:13
  348.4 9.5 %collective-permute-start = (bf16[128,1024]{1,0:T(8,128)(2,1)S(1)}, bf16[128,1024]{1,0:T(8,128)(2,1)S(1)}, u32[]{:S(2)}, u32[]{:S(2)}) collective-permute-start(bf16[128,1024]{1,0:T(8,128)(2,1)S(1)} %convert_element_type.146), channel_id=1, source_target_pairs={{15,0},{0,1},{1,2},{2,3},{3,4},{4,5},{5,6},{6,7},{7,8},{8,9},{9,10... | collective-permute-start | bytes 786440 | tf_op jit(solution)/shard_map/while/body/eval_jaxpr/ppermute | solution.py:13
  358.0 9.5 %collective-permute-start = (bf16[128,1024]{1,0:T(8,128)(2,1)S(1)}, bf16[128,1024]{1,0:T(8,128)(2,1)S(1)}, u32[]{:S(2)}, u32[]{:S(2)}) collective-permute-start(bf16[128,1024]{1,0:T(8,128)(2,1)S(1)} %convert_element_type.146), channel_id=1, source_target_pairs={{15,0},{0,1},{1,2},{2,3},{3,4},{4,5},{5,6},{6,7},{7,8},{8,9},{9,10... | collective-permute-start | bytes 786440 | tf_op jit(solution)/shard_map/while/body/eval_jaxpr/ppermute | solution.py:13
  367.6 9.5 %collective-permute-start = (bf16[128,1024]{1,0:T(8,128)(2,1)S(1)}, bf16[128,1024]{1,0:T(8,128)(2,1)S(1)}, u32[]{:S(2)}, u32[]{:S(2)}) collective-permute-start(bf16[128,1024]{1,0:T(8,128)(2,1)S(1)} %convert_element_type.146), channel_id=1, source_target_pairs={{15,0},{0,1},{1,2},{2,3},{3,4},{4,5},{5,6},{6,7},{7,8},{8,9},{9,10... | collective-permute-start | bytes 786440 | tf_op jit(solution)/shard_map/while/body/eval_jaxpr/ppermute | solution.py:13
  377.3 9.5 %collective-permute-start = (bf16[128,1024]{1,0:T(8,128)(2,1)S(1)}, bf16[128,1024]{1,0:T(8,128)(2,1)S(1)}, u32[]{:S(2)}, u32[]{:S(2)}) collective-permute-start(bf16[128,1024]{1,0:T(8,128)(2,1)S(1)} %convert_element_type.146), channel_id=1, source_target_pairs={{15,0},{0,1},{1,2},{2,3},{3,4},{4,5},{5,6},{6,7},{7,8},{8,9},{9,10... | collective-permute-start | bytes 786440 | tf_op jit(solution)/shard_map/while/body/eval_jaxpr/ppermute | solution.py:13
  386.9 9.5 %collective-permute-start = (bf16[128,1024]{1,0:T(8,128)(2,1)S(1)}, bf16[128,1024]{1,0:T(8,128)(2,1)S(1)}, u32[]{:S(2)}, u32[]{:S(2)}) collective-permute-start(bf16[128,1024]{1,0:T(8,128)(2,1)S(1)} %convert_element_type.146), channel_id=1, source_target_pairs={{15,0},{0,1},{1,2},{2,3},{3,4},{4,5},{5,6},{6,7},{7,8},{8,9},{9,10... | collective-permute-start | bytes 786440 | tf_op jit(solution)/shard_map/while/body/eval_jaxpr/ppermute | solution.py:13
  396.5 9.5 %collective-permute-start = (bf16[128,1024]{1,0:T(8,128)(2,1)S(1)}, bf16[128,1024]{1,0:T(8,128)(2,1)S(1)}, u32[]{:S(2)}, u32[]{:S(2)}) collective-permute-start(bf16[128,1024]{1,0:T(8,128)(2,1)S(1)} %convert_element_type.146), channel_id=1, source_target_pairs={{15,0},{0,1},{1,2},{2,3},{3,4},{4,5},{5,6},{6,7},{7,8},{8,9},{9,10... | collective-permute-start | bytes 786440 | tf_op jit(solution)/shard_map/while/body/eval_jaxpr/ppermute | solution.py:13
  406.1 9.5 %collective-permute-start = (bf16[128,1024]{1,0:T(8,128)(2,1)S(1)}, bf16[128,1024]{1,0:T(8,128)(2,1)S(1)}, u32[]{:S(2)}, u32[]{:S(2)}) collective-permute-start(bf16[128,1024]{1,0:T(8,128)(2,1)S(1)} %convert_element_type.146), channel_id=1, source_target_pairs={{15,0},{0,1},{1,2},{2,3},{3,4},{4,5},{5,6},{6,7},{7,8},{8,9},{9,10... | collective-permute-start | bytes 786440 | tf_op jit(solution)/shard_map/while/body/eval_jaxpr/ppermute | solution.py:13
  417.5 2.5 copy-start.27
  417.5 3.8 copy-start.3
  423.7 38.3 %copy-start.14 = (bf16[128,512]{1,0:T(8,128)(2,1)S(1)}, bf16[128,512]{1,0:T(8,128)(2,1)}, u32[]{:S(2)}) copy-start(bf16[128,512]{1,0:T(8,128)(2,1)} %copy-done.13) | copy-start | bytes 393220
  423.7 38.3 %copy-start.24 = (f32[128]{0:T(128)S(1)}, f32[128]{0:T(128)}, u32[]{:S(2)}) copy-start(f32[128]{0:T(128)} %copy-done.23) | copy-start | bytes 1540
  423.7 38.3 %copy-start.26 = (f32[128]{0:T(128)S(1)}, f32[128]{0:T(128)}, u32[]{:S(2)}) copy-start(f32[128]{0:T(128)} %copy-done.25) | copy-start | bytes 1540
Sparse Core Ops, SparseCore 0:
  421.4 36.3 reduce-scatter.1
where the time goes:
time: 474 us; the launch traced here: 472 us
  waiting for transfers between devices  262 us (55%)
  local copies, waits for them, and re-layouts  54.7 us (12%)
  other arithmetic  53.8 us (11%)
  matrix products  51.6 us (11%)
  blocking collectives  30.4 us (6%)
  between operations  15.1 us (3%)
    ppermute x31, waiting for transfers between devices, from_behind(): return lax.ppermute(block, axis, route)  262 us
    reduce_sum x16, other arithmetic, slot_terms(): return jnp.sum(jnp.where(matched[:, None, None], grad_slots, 0.0), 0)  31.2 us
    all_gather x1, blocking collectives, local(): lax.all_gather(item_table, 'item', axis=1, tiled=True)  30.4 us
    dot_general x3, matrix products, key_block(): jnp.einsum('hqk,khd->qhd', weights, v_tile, preferred_element_type=jnp.fl...  14 us
    while x15, local copies, waits for them, and re-layouts  10.5 us
  transfers between devices with their start and end apart: 32, of which 31 were waited for; matrix products, arithmetic and copies ran while one was open for 16% of the time, Pallas kernels for 0%

commit v1 on v0

--- a/solution.py
+++ b/solution.py
@@ -138,7 +138,9 @@
     own_hot = (own_ids[:, None] == catalogue[None, :]).astype(jnp.bfloat16)
     cand_emb = jnp.dot(
         own_hot,
-        lax.all_gather(item_table, "item", axis=1, tiled=True),
+        jnp.concatenate(
+            lax.all_to_all(jnp.stack([item_table] * lax.axis_size("item")), "item", 0, 0), axis=1
+        ),
         preferred_element_type=jnp.float32,
     ).astype(jnp.bfloat16)
     projected = jax.nn.silu(jnp.dot(events, w_in, preferred_element_type=jnp.float32)).astype(

time: 474 us -> 451 us (0.951)
  blocking collectives: 30.4 us -> 0 us
  starting transfers between devices: 2.27 us -> 8.6 us
    all_gather x1 -> x0, blocking collectives: 30.4 us -> none  [local(): lax.all_gather(item_table, 'item', axis=1, tiled=True)]
    all_to_all x0 -> x1, starting transfers between devices: none -> 6.32 us  [local(): lax.all_to_all(jnp.stack([item_table] * lax.axis_size('item')), 'item', 0...]
  transfers between devices with their start and end apart: 32 -> 33, of which waited for: 31 -> 31; matrix products, arithmetic and copies ran while one was open for 16% -> 19% of each run, Pallas kernels for 0% -> 0%
where the time goes in v1:
time: 451 us; the launch traced here: 449 us
  waiting for transfers between devices  262 us (58%)
  local copies, waits for them, and re-layouts  56.1 us (12%)
  other arithmetic  53.9 us (12%)
  matrix products  50.6 us (11%)
  between operations  15.1 us (3%)
  starting transfers between devices  8.6 us (2%)
    ppermute x31, waiting for transfers between devices, from_behind(): return lax.ppermute(block, axis, route)  262 us
    reduce_sum x16, other arithmetic, slot_terms(): return jnp.sum(jnp.where(matched[:, None, None], grad_slots, 0.0), 0)  31.2 us
    dot_general x3, matrix products, key_block(): jnp.einsum('hqk,khd->qhd', weights, v_tile, preferred_element_type=jnp.fl...  14 us
    while x15, local copies, waits for them, and re-layouts  10.6 us
  transfers between devices with their start and end apart: 33, of which 31 were waited for; matrix products, arithmetic and copies ran while one was open for 19% of the time, Pallas kernels for 0%

profile of v1, /device:TPU:0, one launch (start us, length us, event | category | flops | bytes accessed | tf_op | source)
XLA Modules:
  0.0 448.6 jit_solution(15856531150567395559)
XLA Ops:
  8.9 6.3 %all-to-all-start = ((bf16[8,384,64]{1,2,0:T(8,128)(2,1)}), bf16[8,384,64]{1,2,0:T(8,128)(2,1)S(1)}, u32[]{:S(2)}, u32[]{:S(2)}) async-start(bf16[8,384,64]{1,2,0:T(8,128)(2,1)} %stack.2), calls=%async_computation | async-start | bytes 786432 | tf_op jit(solution)/shard_map/all_to_all | solution.py:142
  16.0 4.2 multiply_convert_fusion
  20.2 2.1 fusion.61
  22.3 2.3 copy.34
  24.6 2.3 copy.35
  26.9 2.3 copy.36
  34.8 161.6 %while.57 = (s32[]{:T(128)}, bf16[128,1024]{1,0:T(8,128)(2,1)}, bf16[4,128,1024]{2,1,0:T(8,128)(2,1)S(1)}, s32[]{:T(128)}, s32[4]{0:T(128)S(1)}, /*index=5*/s32[]{:T(128)}, s32[]{:T(128)}, s32[]{:T(128)}, s32[]{:T(128)}) while((s32[]{:T(128)}, bf16[128,1024]{1,0:T(8,128)(2,1)}, bf16[4,128,1024]{2,1,0:T(8,128)(2,1)S(1)}, s32[]{:T(128)}, ...), condition=%wide.region_7.8_spmd.clone, body=%wide.region_6.7_spmd.clone.sunk | while | flops 1048595 | bytes 3932460 | solution.py:166
  34.8 9.6 %collective-permute-done.1 = bf16[128,1024]{1,0:T(8,128)(2,1)S(1)} collective-permute-done((bf16[128,1024]{1,0:T(8,128)(2,1)}, bf16[128,1024]{1,0:T(8,128)(2,1)S(1)}, u32[]{:S(2)}, u32[]{:S(2)}) %collective-permute-start.1) | collective-permute-done | bytes 262176 | tf_op jit(solution)/shard_map/while/body/eval_jaxpr/ppermute | solution.py:13
  45.6 9.6 %collective-permute-done.1 = bf16[128,1024]{1,0:T(8,128)(2,1)S(1)} collective-permute-done((bf16[128,1024]{1,0:T(8,128)(2,1)}, bf16[128,1024]{1,0:T(8,128)(2,1)S(1)}, u32[]{:S(2)}, u32[]{:S(2)}) %collective-permute-start.1) | collective-permute-done | bytes 262176 | tf_op jit(solution)/shard_map/while/body/eval_jaxpr/ppermute | solution.py:13
  56.4 9.6 %collective-permute-done.1 = bf16[128,1024]{1,0:T(8,128)(2,1)S(1)} collective-permute-done((bf16[128,1024]{1,0:T(8,128)(2,1)}, bf16[128,1024]{1,0:T(8,128)(2,1)S(1)}, u32[]{:S(2)}, u32[]{:S(2)}) %collective-permute-start.1) | collective-permute-done | bytes 262176 | tf_op jit(solution)/shard_map/while/body/eval_jaxpr/ppermute | solution.py:13
  67.2 9.6 %collective-permute-done.1 = bf16[128,1024]{1,0:T(8,128)(2,1)S(1)} collective-permute-done((bf16[128,1024]{1,0:T(8,128)(2,1)}, bf16[128,1024]{1,0:T(8,128)(2,1)S(1)}, u32[]{:S(2)}, u32[]{:S(2)}) %collective-permute-start.1) | collective-permute-done | bytes 262176 | tf_op jit(solution)/shard_map/while/body/eval_jaxpr/ppermute | solution.py:13
  78.0 9.6 %collective-permute-done.1 = bf16[128,1024]{1,0:T(8,128)(2,1)S(1)} collective-permute-done((bf16[128,1024]{1,0:T(8,128)(2,1)}, bf16[128,1024]{1,0:T(8,128)(2,1)S(1)}, u32[]{:S(2)}, u32[]{:S(2)}) %collective-permute-start.1) | collective-permute-done | bytes 262176 | tf_op jit(solution)/shard_map/while/body/eval_jaxpr/ppermute | solution.py:13
  88.7 9.6 %collective-permute-done.1 = bf16[128,1024]{1,0:T(8,128)(2,1)S(1)} collective-permute-done((bf16[128,1024]{1,0:T(8,128)(2,1)}, bf16[128,1024]{1,0:T(8,128)(2,1)S(1)}, u32[]{:S(2)}, u32[]{:S(2)}) %collective-permute-start.1) | collective-permute-done | bytes 262176 | tf_op jit(solution)/shard_map/while/body/eval_jaxpr/ppermute | solution.py:13
  99.5 9.6 %collective-permute-done.1 = bf16[128,1024]{1,0:T(8,128)(2,1)S(1)} collective-permute-done((bf16[128,1024]{1,0:T(8,128)(2,1)}, bf16[128,1024]{1,0:T(8,128)(2,1)S(1)}, u32[]{:S(2)}, u32[]{:S(2)}) %collective-permute-start.1) | collective-permute-done | bytes 262176 | tf_op jit(solution)/shard_map/while/body/eval_jaxpr/ppermute | solution.py:13
  110.3 9.6 %collective-permute-done.1 = bf16[128,1024]{1,0:T(8,128)(2,1)S(1)} collective-permute-done((bf16[128,1024]{1,0:T(8,128)(2,1)}, bf16[128,1024]{1,0:T(8,128)(2,1)S(1)}, u32[]{:S(2)}, u32[]{:S(2)}) %collective-permute-start.1) | collective-permute-done | bytes 262176 | tf_op jit(solution)/shard_map/while/body/eval_jaxpr/ppermute | solution.py:13
  121.1 9.6 %collective-permute-done.1 = bf16[128,1024]{1,0:T(8,128)(2,1)S(1)} collective-permute-done((bf16[128,1024]{1,0:T(8,128)(2,1)}, bf16[128,1024]{1,0:T(8,128)(2,1)S(1)}, u32[]{:S(2)}, u32[]{:S(2)}) %collective-permute-start.1) | collective-permute-done | bytes 262176 | tf_op jit(solution)/shard_map/while/body/eval_jaxpr/ppermute | solution.py:13
  131.8 9.6 %collective-permute-done.1 = bf16[128,1024]{1,0:T(8,128)(2,1)S(1)} collective-permute-done((bf16[128,1024]{1,0:T(8,128)(2,1)}, bf16[128,1024]{1,0:T(8,128)(2,1)S(1)}, u32[]{:S(2)}, u32[]{:S(2)}) %collective-permute-start.1) | collective-permute-done | bytes 262176 | tf_op jit(solution)/shard_map/while/body/eval_jaxpr/ppermute | solution.py:13
  142.6 9.6 %collective-permute-done.1 = bf16[128,1024]{1,0:T(8,128)(2,1)S(1)} collective-permute-done((bf16[128,1024]{1,0:T(8,128)(2,1)}, bf16[128,1024]{1,0:T(8,128)(2,1)S(1)}, u32[]{:S(2)}, u32[]{:S(2)}) %collective-permute-start.1) | collective-permute-done | bytes 262176 | tf_op jit(solution)/shard_map/while/body/eval_jaxpr/ppermute | solution.py:13
  153.4 9.6 %collective-permute-done.1 = bf16[128,1024]{1,0:T(8,128)(2,1)S(1)} collective-permute-done((bf16[128,1024]{1,0:T(8,128)(2,1)}, bf16[128,1024]{1,0:T(8,128)(2,1)S(1)}, u32[]{:S(2)}, u32[]{:S(2)}) %collective-permute-start.1) | collective-permute-done | bytes 262176 | tf_op jit(solution)/shard_map/while/body/eval_jaxpr/ppermute | solution.py:13
  164.2 9.6 %collective-permute-done.1 = bf16[128,1024]{1,0:T(8,128)(2,1)S(1)} collective-permute-done((bf16[128,1024]{1,0:T(8,128)(2,1)}, bf16[128,1024]{1,0:T(8,128)(2,1)S(1)}, u32[]{:S(2)}, u32[]{:S(2)}) %collective-permute-start.1) | collective-permute-done | bytes 262176 | tf_op jit(solution)/shard_map/while/body/eval_jaxpr/ppermute | solution.py:13
  175.0 9.6 %collective-permute-done.1 = bf16[128,1024]{1,0:T(8,128)(2,1)S(1)} collective-permute-done((bf16[128,1024]{1,0:T(8,128)(2,1)}, bf16[128,1024]{1,0:T(8,128)(2,1)S(1)}, u32[]{:S(2)}, u32[]{:S(2)}) %collective-permute-start.1) | collective-permute-done | bytes 262176 | tf_op jit(solution)/shard_map/while/body/eval_jaxpr/ppermute | solution.py:13
  185.7 9.6 %collective-permute-done.1 = bf16[128,1024]{1,0:T(8,128)(2,1)S(1)} collective-permute-done((bf16[128,1024]{1,0:T(8,128)(2,1)}, bf16[128,1024]{1,0:T(8,128)(2,1)S(1)}, u32[]{:S(2)}, u32[]{:S(2)}) %collective-permute-start.1) | collective-permute-done | bytes 262176 | tf_op jit(solution)/shard_map/while/body/eval_jaxpr/ppermute | solution.py:13
  201.7 6.4 %select_convert_fusion = (bf16[8,128,1664]{2,1,0:T(8,128)(2,1)S(1)}, f32[8,128,1664]{2,1,0:T(8,128)}) fusion(pred[1664]{0:T(1024)(128)(4,1)S(1)} %concatenate.35, bf16[128,8,64]{0,2,1:T(8,128)(2,1)S(1)} %bitcast.124, bf16[512,8,64]{0,2,1:T(8,128)(2,1)S(1)} %concatenate.37, bf16[128,8,64]{0,2,1:T(8,128)(2,1)S(1)} %bitcast.129, bf16[1024,8,64]{0,2,1:T(8,128)(2,1)} %bitcast.118), kind=kOutput, calls=%fused_computation.43 | convolution fusion | flops 235143168 | bytes 12060288 | tf_op jit(solution)/shard_map/qhd,khd->hqk/dot_general | solution.py:86
  208.1 2.1 fusion.65
  217.1 6.2 %multiply_convert_fusion.1 = bf16[8,128,1664]{2,1,0:T(8,128)(2,1)S(1)} fusion(f32[8,128,1664]{2,1,0:T(8,128)} %get-tuple-element.502, bf16[128,8,64]{0,2,1:T(8,128)(2,1)S(1)} %bitcast.127, pred[1664]{0:T(1024)(128)(4,1)S(1)} %concatenate.35, bf16[512,8,64]{0,2,1:T(8,128)(2,1)} %concatenate.33, bf16[128,8,64]{0,2,1:T(8,128)(2,1)} %bitcast.131, ...), kind=kOutput, calls=%fused_computation.42 | convolution fusion | flops 243662848 | bytes 12060288 | tf_op jit(solution)/shard_map/qhd,khd->hqk/dot_general | solution.py:108
  225.7 2.1 fusion.36
  231.8 2.6 copy.48
  238.2 3.1 pad_maximum_fusion
  241.4 153.7 %while.56 = (s32[]{:T(128)}, f32[128,1024]{1,0:T(8,128)S(1)}, s32[]{:T(128)}, s32[4]{0:T(128)S(1)}, f32[4,128,1024]{2,1,0:T(8,128)}, /*index=5*/s32[]{:T(128)}, s32[]{:T(128)}, s32[]{:T(128)}, s32[]{:T(128)}) while((s32[]{:T(128)}, f32[128,1024]{1,0:T(8,128)S(1)}, s32[]{:T(128)}, s32[4]{0:T(128)S(1)}, f32[4,128,1024]{2,1,0:T(8,128)}, ...), condition=%wide.region_14.15_spmd, body=%wide.region_12.14_spmd.sunk | while | flops 1310738 | bytes 5767450 | solution.py:195
  241.5 1.9 select_reduce_fusion.2
  243.5 7.4 %collective-permute-done = bf16[128,1024]{1,0:T(8,128)(2,1)S(1)} collective-permute-done((bf16[128,1024]{1,0:T(8,128)(2,1)S(1)}, bf16[128,1024]{1,0:T(8,128)(2,1)S(1)}, u32[]{:S(2)}, u32[]{:S(2)}) %collective-permute-start) | collective-permute-done | bytes 262176 | tf_op jit(solution)/shard_map/while/body/eval_jaxpr/ppermute | solution.py:13
  253.1 7.4 %collective-permute-done = bf16[128,1024]{1,0:T(8,128)(2,1)S(1)} collective-permute-done((bf16[128,1024]{1,0:T(8,128)(2,1)S(1)}, bf16[128,1024]{1,0:T(8,128)(2,1)S(1)}, u32[]{:S(2)}, u32[]{:S(2)}) %collective-permute-start) | collective-permute-done | bytes 262176 | tf_op jit(solution)/shard_map/while/body/eval_jaxpr/ppermute | solution.py:13
  262.7 7.4 %collective-permute-done = bf16[128,1024]{1,0:T(8,128)(2,1)S(1)} collective-permute-done((bf16[128,1024]{1,0:T(8,128)(2,1)S(1)}, bf16[128,1024]{1,0:T(8,128)(2,1)S(1)}, u32[]{:S(2)}, u32[]{:S(2)}) %collective-permute-start) | collective-permute-done | bytes 262176 | tf_op jit(solution)/shard_map/while/body/eval_jaxpr/ppermute | solution.py:13
  270.3 1.9 select_reduce_fusion.2
  272.3 7.4 %collective-permute-done = bf16[128,1024]{1,0:T(8,128)(2,1)S(1)} collective-permute-done((bf16[128,1024]{1,0:T(8,128)(2,1)S(1)}, bf16[128,1024]{1,0:T(8,128)(2,1)S(1)}, u32[]{:S(2)}, u32[]{:S(2)}) %collective-permute-start) | collective-permute-done | bytes 262176 | tf_op jit(solution)/shard_map/while/body/eval_jaxpr/ppermute | solution.py:13
  280.0 1.9 select_reduce_fusion.2
  281.9 7.4 %collective-permute-done = bf16[128,1024]{1,0:T(8,128)(2,1)S(1)} collective-permute-done((bf16[128,1024]{1,0:T(8,128)(2,1)S(1)}, bf16[128,1024]{1,0:T(8,128)(2,1)S(1)}, u32[]{:S(2)}, u32[]{:S(2)}) %collective-permute-start) | collective-permute-done | bytes 262176 | tf_op jit(solution)/shard_map/while/body/eval_jaxpr/ppermute | solution.py:13
  291.5 7.4 %collective-permute-done = bf16[128,1024]{1,0:T(8,128)(2,1)S(1)} collective-permute-done((bf16[128,1024]{1,0:T(8,128)(2,1)S(1)}, bf16[128,1024]{1,0:T(8,128)(2,1)S(1)}, u32[]{:S(2)}, u32[]{:S(2)}) %collective-permute-start) | collective-permute-done | bytes 262176 | tf_op jit(solution)/shard_map/while/body/eval_jaxpr/ppermute | solution.py:13
  301.1 7.4 %collective-permute-done = bf16[128,1024]{1,0:T(8,128)(2,1)S(1)} collective-permute-done((bf16[128,1024]{1,0:T(8,128)(2,1)S(1)}, bf16[128,1024]{1,0:T(8,128)(2,1)S(1)}, u32[]{:S(2)}, u32[]{:S(2)}) %collective-permute-start) | collective-permute-done | bytes 262176 | tf_op jit(solution)/shard_map/while/body/eval_jaxpr/ppermute | solution.py:13
  308.8 1.9 select_reduce_fusion.2
  310.7 7.4 %collective-permute-done = bf16[128,1024]{1,0:T(8,128)(2,1)S(1)} collective-permute-done((bf16[128,1024]{1,0:T(8,128)(2,1)S(1)}, bf16[128,1024]{1,0:T(8,128)(2,1)S(1)}, u32[]{:S(2)}, u32[]{:S(2)}) %collective-permute-start) | collective-permute-done | bytes 262176 | tf_op jit(solution)/shard_map/while/body/eval_jaxpr/ppermute | solution.py:13
  320.3 7.4 %collective-permute-done = bf16[128,1024]{1,0:T(8,128)(2,1)S(1)} collective-permute-done((bf16[128,1024]{1,0:T(8,128)(2,1)S(1)}, bf16[128,1024]{1,0:T(8,128)(2,1)S(1)}, u32[]{:S(2)}, u32[]{:S(2)}) %collective-permute-start) | collective-permute-done | bytes 262176 | tf_op jit(solution)/shard_map/while/body/eval_jaxpr/ppermute | solution.py:13
  329.9 7.4 %collective-permute-done = bf16[128,1024]{1,0:T(8,128)(2,1)S(1)} collective-permute-done((bf16[128,1024]{1,0:T(8,128)(2,1)S(1)}, bf16[128,1024]{1,0:T(8,128)(2,1)S(1)}, u32[]{:S(2)}, u32[]{:S(2)}) %collective-permute-start) | collective-permute-done | bytes 262176 | tf_op jit(solution)/shard_map/while/body/eval_jaxpr/ppermute | solution.py:13
  339.6 7.4 %collective-permute-done = bf16[128,1024]{1,0:T(8,128)(2,1)S(1)} collective-permute-done((bf16[128,1024]{1,0:T(8,128)(2,1)S(1)}, bf16[128,1024]{1,0:T(8,128)(2,1)S(1)}, u32[]{:S(2)}, u32[]{:S(2)}) %collective-permute-start) | collective-permute-done | bytes 262176 | tf_op jit(solution)/shard_map/while/body/eval_jaxpr/ppermute | solution.py:13
  347.2 1.9 select_reduce_fusion.2
  349.2 7.4 %collective-permute-done = bf16[128,1024]{1,0:T(8,128)(2,1)S(1)} collective-permute-done((bf16[128,1024]{1,0:T(8,128)(2,1)S(1)}, bf16[128,1024]{1,0:T(8,128)(2,1)S(1)}, u32[]{:S(2)}, u32[]{:S(2)}) %collective-permute-start) | collective-permute-done | bytes 262176 | tf_op jit(solution)/shard_map/while/body/eval_jaxpr/ppermute | solution.py:13
  358.8 7.4 %collective-permute-done = bf16[128,1024]{1,0:T(8,128)(2,1)S(1)} collective-permute-done((bf16[128,1024]{1,0:T(8,128)(2,1)S(1)}, bf16[128,1024]{1,0:T(8,128)(2,1)S(1)}, u32[]{:S(2)}, u32[]{:S(2)}) %collective-permute-start) | collective-permute-done | bytes 262176 | tf_op jit(solution)/shard_map/while/body/eval_jaxpr/ppermute | solution.py:13
  368.4 7.4 %collective-permute-done = bf16[128,1024]{1,0:T(8,128)(2,1)S(1)} collective-permute-done((bf16[128,1024]{1,0:T(8,128)(2,1)S(1)}, bf16[128,1024]{1,0:T(8,128)(2,1)S(1)}, u32[]{:S(2)}, u32[]{:S(2)}) %collective-permute-start) | collective-permute-done | bytes 262176 | tf_op jit(solution)/shard_map/while/body/eval_jaxpr/ppermute | solution.py:13
  376.0 1.9 select_reduce_fusion.2
  378.0 7.4 %collective-permute-done = bf16[128,1024]{1,0:T(8,128)(2,1)S(1)} collective-permute-done((bf16[128,1024]{1,0:T(8,128)(2,1)S(1)}, bf16[128,1024]{1,0:T(8,128)(2,1)S(1)}, u32[]{:S(2)}, u32[]{:S(2)}) %collective-permute-start) | collective-permute-done | bytes 262176 | tf_op jit(solution)/shard_map/while/body/eval_jaxpr/ppermute | solution.py:13
  385.6 1.9 select_reduce_fusion.2
  387.6 7.4 %collective-permute-done = bf16[128,1024]{1,0:T(8,128)(2,1)S(1)} collective-permute-done((bf16[128,1024]{1,0:T(8,128)(2,1)S(1)}, bf16[128,1024]{1,0:T(8,128)(2,1)S(1)}, u32[]{:S(2)}, u32[]{:S(2)}) %collective-permute-start) | collective-permute-done | bytes 262176 | tf_op jit(solution)/shard_map/while/body/eval_jaxpr/ppermute | solution.py:13
  395.3 2.1 convolution_add_fusion.1
  399.8 38.4 %while.55 = (s32[]{:T(128)}, bf16[1024,512]{1,0:T(8,128)(2,1)}, s32[]{:T(128)}, s32[]{:T(128)}, bf16[1024,8,64]{0,2,1:T(8,128)(2,1)}, /*index=5*/bf16[1024,8,64]...) while((s32[]{:T(128)}, bf16[1024,512]{1,0:T(8,128)(2,1)}, ...), condition=%wide.region_5.6_spmd, body=%wide.region_0.5_spmd.sunk | while | flops 824184320 | bytes 14710306 | solution.py:72
  401.9 5.6 %while.58 = (s32[]{:T(128)}, f32[512,8,64]{0,2,1:T(8,128)S(1)}, s32[]{:T(128)}, bf16[1024,8,64]{0,2,1:T(8,128)(2,1)}, s32[]{:T(128)}, /*index=5*/bf16[1024,8,64]...) while((s32[]{:T(128)}, f32[512,8,64]{0,2,1:T(8,128)S(1)}, ...), condition=%wide.region_2.2_spmd.clone, body=%wide.region_1.1_spmd.clone.sunk | while | flops 552339456 | bytes 4204731 | solution.py:59
  402.8 4.7 %fusion.100 = f32[512,8,64]{0,2,1:T(8,128)S(1)} fusion(f32[512,8,64]{0,2,1:T(8,128)S(1)} %get-tuple-element.718, pred[512,512]{0,1:T(8,128)(4,1)S(1)} %compare_and_fusion.2, bf16[512,8,64]{0,2,1:T(8,128)(2,1)} %get-tuple-element.735, bf16[1024,8,64]{0,2,1:T(8,128)(2,1)} %get-tuple-element.734, s32[]{:T(128)S(6)} %select_n.127, ...), kind=kOutput, calls=%fused_computation.14.clone.1 | convolution fusion | flops 551813120 | bytes 3933184 | tf_op jit(solution)/shard_map/while/body/while/body/hqk,khd->qhd/dot_general | solution.py:55
  409.4 2.1 copy.53
  413.7 2.5 fusion.95
  418.2 11.3 %while.58 = (s32[]{:T(128)}, f32[512,8,64]{0,2,1:T(8,128)S(1)}, s32[]{:T(128)}, bf16[1024,8,64]{0,2,1:T(8,128)(2,1)}, s32[]{:T(128)}, /*index=5*/bf16[1024,8,64]...) while((s32[]{:T(128)}, f32[512,8,64]{0,2,1:T(8,128)S(1)}, ...), condition=%wide.region_2.2_spmd.clone, body=%wide.region_1.1_spmd.clone.sunk | while | flops 552339456 | bytes 4204731 | solution.py:59
  419.2 4.7 %fusion.100 = f32[512,8,64]{0,2,1:T(8,128)S(1)} fusion(f32[512,8,64]{0,2,1:T(8,128)S(1)} %get-tuple-element.718, pred[512,512]{0,1:T(8,128)(4,1)S(1)} %compare_and_fusion.2, bf16[512,8,64]{0,2,1:T(8,128)(2,1)} %get-tuple-element.735, bf16[1024,8,64]{0,2,1:T(8,128)(2,1)} %get-tuple-element.734, s32[]{:T(128)S(6)} %select_n.127, ...), kind=kOutput, calls=%fused_computation.14.clone.1 | convolution fusion | flops 551813120 | bytes 3933184 | tf_op jit(solution)/shard_map/while/body/while/body/hqk,khd->qhd/dot_general | solution.py:55
  424.8 4.7 %fusion.100 = f32[512,8,64]{0,2,1:T(8,128)S(1)} fusion(f32[512,8,64]{0,2,1:T(8,128)S(1)} %get-tuple-element.718, pred[512,512]{0,1:T(8,128)(4,1)S(1)} %compare_and_fusion.2, bf16[512,8,64]{0,2,1:T(8,128)(2,1)} %get-tuple-element.735, bf16[1024,8,64]{0,2,1:T(8,128)(2,1)} %get-tuple-element.734, s32[]{:T(128)S(6)} %select_n.127, ...), kind=kOutput, calls=%fused_computation.14.clone.1 | convolution fusion | flops 551813120 | bytes 3933184 | tf_op jit(solution)/shard_map/while/body/while/body/hqk,khd->qhd/dot_general | solution.py:55
  431.4 2.1 copy.53
  435.7 2.5 fusion.95
  438.2 2.1 fusion.34
  (263 shorter events, 86.3 us)
Async XLA Ops:
  7.2 8.8 %copy-start = (bf16[512,2048]{1,0:T(8,128)(2,1)S(1)}, bf16[512,2048]{1,0:T(8,128)(2,1)}, u32[]{:S(2)}) copy-start(bf16[512,2048]{1,0:T(8,128)(2,1)} %param.21) | copy-start | bytes 6291460
  8.9 20.3 %all-to-all-start = ((bf16[8,384,64]{1,2,0:T(8,128)(2,1)}), bf16[8,384,64]{1,2,0:T(8,128)(2,1)S(1)}, u32[]{:S(2)}, u32[]{:S(2)}) async-start(bf16[8,384,64]{1,2,0:T(8,128)(2,1)} %stack.2), calls=%async_computation | async-start | bytes 786432 | tf_op jit(solution)/shard_map/all_to_all | solution.py:142
  15.2 425.1 %reduce-scatter.2.cloned.1.call-start = ((), (), s32[]{:S(2)}) async-start(), calls=%async_computation.2 | async-start | bytes 442368 | tf_op jit(solution)/shard_map/reduce_scatter | solution.py:206
  22.3 6.9 %copy-start.26 = (s32[1,128]{1,0:T(1,128)S(1)}, s32[1,128]{1,0:T(1,128)}, u32[]{:S(2)}) copy-start(s32[1,128]{1,0:T(1,128)} %param.18) | copy-start | bytes 1540
  29.5 2.3 copy-start.12
  29.5 5.3 %copy-start.27 = (s32[1,4]{1,0:T(1,128)S(1)}, s32[1,4]{1,0:T(1,128)}, u32[]{:S(2)}) copy-start(s32[1,4]{1,0:T(1,128)} %param.19) | copy-start | bytes 52
  31.0 0.8 copy-start.4
  34.8 9.6 %collective-permute-start.1 = (bf16[128,1024]{1,0:T(8,128)(2,1)}, bf16[128,1024]{1,0:T(8,128)(2,1)S(1)}, u32[]{:S(2)}, u32[]{:S(2)}) collective-permute-start(bf16[128,1024]{1,0:T(8,128)(2,1)} %get-tuple-element.808), channel_id=1, source_target_pairs={{15,0},{0,1},{1,2},{2,3},{3,4},{4,5},{5,6},{6,7},{7,8},{8,9},{9,10... | collective-permute-start | bytes 786440 | tf_op jit(solution)/shard_map/while/body/eval_jaxpr/ppermute | solution.py:13
  45.5 9.7 %collective-permute-start.1 = (bf16[128,1024]{1,0:T(8,128)(2,1)}, bf16[128,1024]{1,0:T(8,128)(2,1)S(1)}, u32[]{:S(2)}, u32[]{:S(2)}) collective-permute-start(bf16[128,1024]{1,0:T(8,128)(2,1)} %get-tuple-element.808), channel_id=1, source_target_pairs={{15,0},{0,1},{1,2},{2,3},{3,4},{4,5},{5,6},{6,7},{7,8},{8,9},{9,10... | collective-permute-start | bytes 786440 | tf_op jit(solution)/shard_map/while/body/eval_jaxpr/ppermute | solution.py:13
  56.3 9.7 %collective-permute-start.1 = (bf16[128,1024]{1,0:T(8,128)(2,1)}, bf16[128,1024]{1,0:T(8,128)(2,1)S(1)}, u32[]{:S(2)}, u32[]{:S(2)}) collective-permute-start(bf16[128,1024]{1,0:T(8,128)(2,1)} %get-tuple-element.808), channel_id=1, source_target_pairs={{15,0},{0,1},{1,2},{2,3},{3,4},{4,5},{5,6},{6,7},{7,8},{8,9},{9,10... | collective-permute-start | bytes 786440 | tf_op jit(solution)/shard_map/while/body/eval_jaxpr/ppermute | solution.py:13
  67.1 9.7 %collective-permute-start.1 = (bf16[128,1024]{1,0:T(8,128)(2,1)}, bf16[128,1024]{1,0:T(8,128)(2,1)S(1)}, u32[]{:S(2)}, u32[]{:S(2)}) collective-permute-start(bf16[128,1024]{1,0:T(8,128)(2,1)} %get-tuple-element.808), channel_id=1, source_target_pairs={{15,0},{0,1},{1,2},{2,3},{3,4},{4,5},{5,6},{6,7},{7,8},{8,9},{9,10... | collective-permute-start | bytes 786440 | tf_op jit(solution)/shard_map/while/body/eval_jaxpr/ppermute | solution.py:13
  77.8 9.7 %collective-permute-start.1 = (bf16[128,1024]{1,0:T(8,128)(2,1)}, bf16[128,1024]{1,0:T(8,128)(2,1)S(1)}, u32[]{:S(2)}, u32[]{:S(2)}) collective-permute-start(bf16[128,1024]{1,0:T(8,128)(2,1)} %get-tuple-element.808), channel_id=1, source_target_pairs={{15,0},{0,1},{1,2},{2,3},{3,4},{4,5},{5,6},{6,7},{7,8},{8,9},{9,10... | collective-permute-start | bytes 786440 | tf_op jit(solution)/shard_map/while/body/eval_jaxpr/ppermute | solution.py:13
  88.6 9.7 %collective-permute-start.1 = (bf16[128,1024]{1,0:T(8,128)(2,1)}, bf16[128,1024]{1,0:T(8,128)(2,1)S(1)}, u32[]{:S(2)}, u32[]{:S(2)}) collective-permute-start(bf16[128,1024]{1,0:T(8,128)(2,1)} %get-tuple-element.808), channel_id=1, source_target_pairs={{15,0},{0,1},{1,2},{2,3},{3,4},{4,5},{5,6},{6,7},{7,8},{8,9},{9,10... | collective-permute-start | bytes 786440 | tf_op jit(solution)/shard_map/while/body/eval_jaxpr/ppermute | solution.py:13
  99.4 9.7 %collective-permute-start.1 = (bf16[128,1024]{1,0:T(8,128)(2,1)}, bf16[128,1024]{1,0:T(8,128)(2,1)S(1)}, u32[]{:S(2)}, u32[]{:S(2)}) collective-permute-start(bf16[128,1024]{1,0:T(8,128)(2,1)} %get-tuple-element.808), channel_id=1, source_target_pairs={{15,0},{0,1},{1,2},{2,3},{3,4},{4,5},{5,6},{6,7},{7,8},{8,9},{9,10... | collective-permute-start | bytes 786440 | tf_op jit(solution)/shard_map/while/body/eval_jaxpr/ppermute | solution.py:13
  110.2 9.7 %collective-permute-start.1 = (bf16[128,1024]{1,0:T(8,128)(2,1)}, bf16[128,1024]{1,0:T(8,128)(2,1)S(1)}, u32[]{:S(2)}, u32[]{:S(2)}) collective-permute-start(bf16[128,1024]{1,0:T(8,128)(2,1)} %get-tuple-element.808), channel_id=1, source_target_pairs={{15,0},{0,1},{1,2},{2,3},{3,4},{4,5},{5,6},{6,7},{7,8},{8,9},{9,10... | collective-permute-start | bytes 786440 | tf_op jit(solution)/shard_map/while/body/eval_jaxpr/ppermute | solution.py:13
  121.0 9.7 %collective-permute-start.1 = (bf16[128,1024]{1,0:T(8,128)(2,1)}, bf16[128,1024]{1,0:T(8,128)(2,1)S(1)}, u32[]{:S(2)}, u32[]{:S(2)}) collective-permute-start(bf16[128,1024]{1,0:T(8,128)(2,1)} %get-tuple-element.808), channel_id=1, source_target_pairs={{15,0},{0,1},{1,2},{2,3},{3,4},{4,5},{5,6},{6,7},{7,8},{8,9},{9,10... | collective-permute-start | bytes 786440 | tf_op jit(solution)/shard_map/while/body/eval_jaxpr/ppermute | solution.py:13
  131.7 9.7 %collective-permute-start.1 = (bf16[128,1024]{1,0:T(8,128)(2,1)}, bf16[128,1024]{1,0:T(8,128)(2,1)S(1)}, u32[]{:S(2)}, u32[]{:S(2)}) collective-permute-start(bf16[128,1024]{1,0:T(8,128)(2,1)} %get-tuple-element.808), channel_id=1, source_target_pairs={{15,0},{0,1},{1,2},{2,3},{3,4},{4,5},{5,6},{6,7},{7,8},{8,9},{9,10... | collective-permute-start | bytes 786440 | tf_op jit(solution)/shard_map/while/body/eval_jaxpr/ppermute | solution.py:13
  142.5 9.7 %collective-permute-start.1 = (bf16[128,1024]{1,0:T(8,128)(2,1)}, bf16[128,1024]{1,0:T(8,128)(2,1)S(1)}, u32[]{:S(2)}, u32[]{:S(2)}) collective-permute-start(bf16[128,1024]{1,0:T(8,128)(2,1)} %get-tuple-element.808), channel_id=1, source_target_pairs={{15,0},{0,1},{1,2},{2,3},{3,4},{4,5},{5,6},{6,7},{7,8},{8,9},{9,10... | collective-permute-start | bytes 786440 | tf_op jit(solution)/shard_map/while/body/eval_jaxpr/ppermute | solution.py:13
  153.3 9.7 %collective-permute-start.1 = (bf16[128,1024]{1,0:T(8,128)(2,1)}, bf16[128,1024]{1,0:T(8,128)(2,1)S(1)}, u32[]{:S(2)}, u32[]{:S(2)}) collective-permute-start(bf16[128,1024]{1,0:T(8,128)(2,1)} %get-tuple-element.808), channel_id=1, source_target_pairs={{15,0},{0,1},{1,2},{2,3},{3,4},{4,5},{5,6},{6,7},{7,8},{8,9},{9,10... | collective-permute-start | bytes 786440 | tf_op jit(solution)/shard_map/while/body/eval_jaxpr/ppermute | solution.py:13
  164.1 9.7 %collective-permute-start.1 = (bf16[128,1024]{1,0:T(8,128)(2,1)}, bf16[128,1024]{1,0:T(8,128)(2,1)S(1)}, u32[]{:S(2)}, u32[]{:S(2)}) collective-permute-start(bf16[128,1024]{1,0:T(8,128)(2,1)} %get-tuple-element.808), channel_id=1, source_target_pairs={{15,0},{0,1},{1,2},{2,3},{3,4},{4,5},{5,6},{6,7},{7,8},{8,9},{9,10... | collective-permute-start | bytes 786440 | tf_op jit(solution)/shard_map/while/body/eval_jaxpr/ppermute | solution.py:13
  174.8 9.7 %collective-permute-start.1 = (bf16[128,1024]{1,0:T(8,128)(2,1)}, bf16[128,1024]{1,0:T(8,128)(2,1)S(1)}, u32[]{:S(2)}, u32[]{:S(2)}) collective-permute-start(bf16[128,1024]{1,0:T(8,128)(2,1)} %get-tuple-element.808), channel_id=1, source_target_pairs={{15,0},{0,1},{1,2},{2,3},{3,4},{4,5},{5,6},{6,7},{7,8},{8,9},{9,10... | collective-permute-start | bytes 786440 | tf_op jit(solution)/shard_map/while/body/eval_jaxpr/ppermute | solution.py:13
  185.6 9.7 %collective-permute-start.1 = (bf16[128,1024]{1,0:T(8,128)(2,1)}, bf16[128,1024]{1,0:T(8,128)(2,1)S(1)}, u32[]{:S(2)}, u32[]{:S(2)}) collective-permute-start(bf16[128,1024]{1,0:T(8,128)(2,1)} %get-tuple-element.808), channel_id=1, source_target_pairs={{15,0},{0,1},{1,2},{2,3},{3,4},{4,5},{5,6},{6,7},{7,8},{8,9},{9,10... | collective-permute-start | bytes 786440 | tf_op jit(solution)/shard_map/while/body/eval_jaxpr/ppermute | solution.py:13
  196.4 5.3 %copy-start.14 = (bf16[128,512]{0,1:T(8,128)(2,1)S(1)}, bf16[128,512]{0,1:T(8,128)(2,1)}, u32[]{:S(2)}) copy-start(bf16[128,512]{0,1:T(8,128)(2,1)} %copy.40) | copy-start | bytes 393220
  196.4 5.3 %copy-start.19 = (bf16[128,512]{0,1:T(8,128)(2,1)S(1)}, bf16[128,512]{0,1:T(8,128)(2,1)}, u32[]{:S(2)}) copy-start(bf16[128,512]{0,1:T(8,128)(2,1)} %copy.41) | copy-start | bytes 393220
  199.1 9.0 %copy-start.9 = (bf16[512,8,64]{0,2,1:T(8,128)(2,1)}, bf16[512,8,64]{0,2,1:T(8,128)(2,1)S(1)}, u32[]{:S(2)}) copy-start(bf16[512,8,64]{0,2,1:T(8,128)(2,1)S(1)} %concatenate.37) | copy-start | bytes 1572868
  201.7 6.4 %copy-start.6 = (bf16[1024,512]{0,1:T(8,128)(2,1)S(1)}, bf16[1024,512]{0,1:T(8,128)(2,1)}, u32[]{:S(2)}) copy-start(bf16[1024,512]{0,1:T(8,128)(2,1)} %copy.35) | copy-start | bytes 3145732
  201.7 6.4 %copy-start.11 = (bf16[512,8,64]{0,2,1:T(8,128)(2,1)S(1)}, bf16[512,8,64]{0,2,1:T(8,128)(2,1)}, u32[]{:S(2)}) copy-start(bf16[512,8,64]{0,2,1:T(8,128)(2,1)} %concatenate.33) | copy-start | bytes 1572868
  201.7 6.4 %copy-start.21 = (bf16[128,512]{0,1:T(8,128)(2,1)S(1)}, bf16[128,512]{0,1:T(8,128)(2,1)}, u32[]{:S(2)}) copy-start(bf16[128,512]{0,1:T(8,128)(2,1)} %copy.38) | copy-start | bytes 393220
  208.1 2.1 copy-start.16
  208.1 4.3 copy-start.3
  208.1 4.3 copy-start.5
  211.3 4.1 copy-start.2
  211.3 3.3 copy-start.22
  212.4 2.2 copy-start.24
  215.4 1.8 copy-start.15
  217.1 6.2 %copy-start.1 = (f32[640,8,64]{0,2,1:T(8,128)}, f32[640,8,64]{0,2,1:T(8,128)S(1)}, u32[]{:S(2)}) copy-start(f32[640,8,64]{0,2,1:T(8,128)S(1)} %convolution_bitcast_fusion) | copy-start | bytes 3932164
  223.4 2.3 copy-start.7
  223.4 2.3 copy-start.10
  223.4 2.3 copy-start.20
  225.7 2.1 slice-start
  225.7 4.8 %slice-start.1 = ((f32[640,8,64]{0,2,1:T(8,128)}), f32[512,8,64]{0,2,1:T(8,128)S(1)}, s32[]{:S(2)}) async-start(f32[640,8,64]{0,2,1:T(8,128)} %copy-done.1), calls=%async_computation.4 | async-start | bytes 2097152 | tf_op jit(solution)/shard_map/slice | solution.py:182
  231.8 5.5 %copy-start.8 = (f32[128,512]{1,0:T(8,128)S(1)}, f32[128,512]{1,0:T(8,128)}, u32[]{:S(2)}) copy-start(f32[128,512]{1,0:T(8,128)} %copy.46) | copy-start | bytes 786436
  241.4 153.8 %copy-start.17 = (f32[8,64,128]{2,1,0:T(8,128)S(1)}, f32[8,64,128]{2,1,0:T(8,128)}, u32[]{:S(2)}) copy-start(f32[8,64,128]{2,1,0:T(8,128)} %fusion.36) | copy-start | bytes 786436
  241.4 153.9 %copy-start.18 = (bf16[1,128,512]{2,1,0:T(8,128)(2,1)S(1)}, bf16[1,128,512]{2,1,0:T(8,128)(2,1)}, u32[]{:S(2)}) copy-start(bf16[1,128,512]{2,1,0:T(8,128)(2,1)} %param.23) | copy-start | bytes 393220
  241.4 9.5 %collective-permute-start = (bf16[128,1024]{1,0:T(8,128)(2,1)S(1)}, bf16[128,1024]{1,0:T(8,128)(2,1)S(1)}, u32[]{:S(2)}, u32[]{:S(2)}) collective-permute-start(bf16[128,1024]{1,0:T(8,128)(2,1)S(1)} %convert_element_type.146), channel_id=1, source_target_pairs={{15,0},{0,1},{1,2},{2,3},{3,4},{4,5},{5,6},{6,7},{7,8},{8,9},{9,10... | collective-permute-start | bytes 786440 | tf_op jit(solution)/shard_map/while/body/eval_jaxpr/ppermute | solution.py:13
  251.0 9.5 %collective-permute-start = (bf16[128,1024]{1,0:T(8,128)(2,1)S(1)}, bf16[128,1024]{1,0:T(8,128)(2,1)S(1)}, u32[]{:S(2)}, u32[]{:S(2)}) collective-permute-start(bf16[128,1024]{1,0:T(8,128)(2,1)S(1)} %convert_element_type.146), channel_id=1, source_target_pairs={{15,0},{0,1},{1,2},{2,3},{3,4},{4,5},{5,6},{6,7},{7,8},{8,9},{9,10... | collective-permute-start | bytes 786440 | tf_op jit(solution)/shard_map/while/body/eval_jaxpr/ppermute | solution.py:13
  260.6 9.5 %collective-permute-start = (bf16[128,1024]{1,0:T(8,128)(2,1)S(1)}, bf16[128,1024]{1,0:T(8,128)(2,1)S(1)}, u32[]{:S(2)}, u32[]{:S(2)}) collective-permute-start(bf16[128,1024]{1,0:T(8,128)(2,1)S(1)} %convert_element_type.146), channel_id=1, source_target_pairs={{15,0},{0,1},{1,2},{2,3},{3,4},{4,5},{5,6},{6,7},{7,8},{8,9},{9,10... | collective-permute-start | bytes 786440 | tf_op jit(solution)/shard_map/while/body/eval_jaxpr/ppermute | solution.py:13
  270.2 9.5 %collective-permute-start = (bf16[128,1024]{1,0:T(8,128)(2,1)S(1)}, bf16[128,1024]{1,0:T(8,128)(2,1)S(1)}, u32[]{:S(2)}, u32[]{:S(2)}) collective-permute-start(bf16[128,1024]{1,0:T(8,128)(2,1)S(1)} %convert_element_type.146), channel_id=1, source_target_pairs={{15,0},{0,1},{1,2},{2,3},{3,4},{4,5},{5,6},{6,7},{7,8},{8,9},{9,10... | collective-permute-start | bytes 786440 | tf_op jit(solution)/shard_map/while/body/eval_jaxpr/ppermute | solution.py:13
  279.8 9.5 %collective-permute-start = (bf16[128,1024]{1,0:T(8,128)(2,1)S(1)}, bf16[128,1024]{1,0:T(8,128)(2,1)S(1)}, u32[]{:S(2)}, u32[]{:S(2)}) collective-permute-start(bf16[128,1024]{1,0:T(8,128)(2,1)S(1)} %convert_element_type.146), channel_id=1, source_target_pairs={{15,0},{0,1},{1,2},{2,3},{3,4},{4,5},{5,6},{6,7},{7,8},{8,9},{9,10... | collective-permute-start | bytes 786440 | tf_op jit(solution)/shard_map/while/body/eval_jaxpr/ppermute | solution.py:13
  289.4 9.5 %collective-permute-start = (bf16[128,1024]{1,0:T(8,128)(2,1)S(1)}, bf16[128,1024]{1,0:T(8,128)(2,1)S(1)}, u32[]{:S(2)}, u32[]{:S(2)}) collective-permute-start(bf16[128,1024]{1,0:T(8,128)(2,1)S(1)} %convert_element_type.146), channel_id=1, source_target_pairs={{15,0},{0,1},{1,2},{2,3},{3,4},{4,5},{5,6},{6,7},{7,8},{8,9},{9,10... | collective-permute-start | bytes 786440 | tf_op jit(solution)/shard_map/while/body/eval_jaxpr/ppermute | solution.py:13
  299.1 9.5 %collective-permute-start = (bf16[128,1024]{1,0:T(8,128)(2,1)S(1)}, bf16[128,1024]{1,0:T(8,128)(2,1)S(1)}, u32[]{:S(2)}, u32[]{:S(2)}) collective-permute-start(bf16[128,1024]{1,0:T(8,128)(2,1)S(1)} %convert_element_type.146), channel_id=1, source_target_pairs={{15,0},{0,1},{1,2},{2,3},{3,4},{4,5},{5,6},{6,7},{7,8},{8,9},{9,10... | collective-permute-start | bytes 786440 | tf_op jit(solution)/shard_map/while/body/eval_jaxpr/ppermute | solution.py:13
  308.7 9.5 %collective-permute-start = (bf16[128,1024]{1,0:T(8,128)(2,1)S(1)}, bf16[128,1024]{1,0:T(8,128)(2,1)S(1)}, u32[]{:S(2)}, u32[]{:S(2)}) collective-permute-start(bf16[128,1024]{1,0:T(8,128)(2,1)S(1)} %convert_element_type.146), channel_id=1, source_target_pairs={{15,0},{0,1},{1,2},{2,3},{3,4},{4,5},{5,6},{6,7},{7,8},{8,9},{9,10... | collective-permute-start | bytes 786440 | tf_op jit(solution)/shard_map/while/body/eval_jaxpr/ppermute | solution.py:13
  318.3 9.5 %collective-permute-start = (bf16[128,1024]{1,0:T(8,128)(2,1)S(1)}, bf16[128,1024]{1,0:T(8,128)(2,1)S(1)}, u32[]{:S(2)}, u32[]{:S(2)}) collective-permute-start(bf16[128,1024]{1,0:T(8,128)(2,1)S(1)} %convert_element_type.146), channel_id=1, source_target_pairs={{15,0},{0,1},{1,2},{2,3},{3,4},{4,5},{5,6},{6,7},{7,8},{8,9},{9,10... | collective-permute-start | bytes 786440 | tf_op jit(solution)/shard_map/while/body/eval_jaxpr/ppermute | solution.py:13
  327.9 9.5 %collective-permute-start = (bf16[128,1024]{1,0:T(8,128)(2,1)S(1)}, bf16[128,1024]{1,0:T(8,128)(2,1)S(1)}, u32[]{:S(2)}, u32[]{:S(2)}) collective-permute-start(bf16[128,1024]{1,0:T(8,128)(2,1)S(1)} %convert_element_type.146), channel_id=1, source_target_pairs={{15,0},{0,1},{1,2},{2,3},{3,4},{4,5},{5,6},{6,7},{7,8},{8,9},{9,10... | collective-permute-start | bytes 786440 | tf_op jit(solution)/shard_map/while/body/eval_jaxpr/ppermute | solution.py:13
  337.5 9.5 %collective-permute-start = (bf16[128,1024]{1,0:T(8,128)(2,1)S(1)}, bf16[128,1024]{1,0:T(8,128)(2,1)S(1)}, u32[]{:S(2)}, u32[]{:S(2)}) collective-permute-start(bf16[128,1024]{1,0:T(8,128)(2,1)S(1)} %convert_element_type.146), channel_id=1, source_target_pairs={{15,0},{0,1},{1,2},{2,3},{3,4},{4,5},{5,6},{6,7},{7,8},{8,9},{9,10... | collective-permute-start | bytes 786440 | tf_op jit(solution)/shard_map/while/body/eval_jaxpr/ppermute | solution.py:13
  347.1 9.5 %collective-permute-start = (bf16[128,1024]{1,0:T(8,128)(2,1)S(1)}, bf16[128,1024]{1,0:T(8,128)(2,1)S(1)}, u32[]{:S(2)}, u32[]{:S(2)}) collective-permute-start(bf16[128,1024]{1,0:T(8,128)(2,1)S(1)} %convert_element_type.146), channel_id=1, source_target_pairs={{15,0},{0,1},{1,2},{2,3},{3,4},{4,5},{5,6},{6,7},{7,8},{8,9},{9,10... | collective-permute-start | bytes 786440 | tf_op jit(solution)/shard_map/while/body/eval_jaxpr/ppermute | solution.py:13
  356.7 9.5 %collective-permute-start = (bf16[128,1024]{1,0:T(8,128)(2,1)S(1)}, bf16[128,1024]{1,0:T(8,128)(2,1)S(1)}, u32[]{:S(2)}, u32[]{:S(2)}) collective-permute-start(bf16[128,1024]{1,0:T(8,128)(2,1)S(1)} %convert_element_type.146), channel_id=1, source_target_pairs={{15,0},{0,1},{1,2},{2,3},{3,4},{4,5},{5,6},{6,7},{7,8},{8,9},{9,10... | collective-permute-start | bytes 786440 | tf_op jit(solution)/shard_map/while/body/eval_jaxpr/ppermute | solution.py:13
  366.3 9.5 %collective-permute-start = (bf16[128,1024]{1,0:T(8,128)(2,1)S(1)}, bf16[128,1024]{1,0:T(8,128)(2,1)S(1)}, u32[]{:S(2)}, u32[]{:S(2)}) collective-permute-start(bf16[128,1024]{1,0:T(8,128)(2,1)S(1)} %convert_element_type.146), channel_id=1, source_target_pairs={{15,0},{0,1},{1,2},{2,3},{3,4},{4,5},{5,6},{6,7},{7,8},{8,9},{9,10... | collective-permute-start | bytes 786440 | tf_op jit(solution)/shard_map/while/body/eval_jaxpr/ppermute | solution.py:13
  375.9 9.5 %collective-permute-start = (bf16[128,1024]{1,0:T(8,128)(2,1)S(1)}, bf16[128,1024]{1,0:T(8,128)(2,1)S(1)}, u32[]{:S(2)}, u32[]{:S(2)}) collective-permute-start(bf16[128,1024]{1,0:T(8,128)(2,1)S(1)} %convert_element_type.146), channel_id=1, source_target_pairs={{15,0},{0,1},{1,2},{2,3},{3,4},{4,5},{5,6},{6,7},{7,8},{8,9},{9,10... | collective-permute-start | bytes 786440 | tf_op jit(solution)/shard_map/while/body/eval_jaxpr/ppermute | solution.py:13
  385.5 9.5 %collective-permute-start = (bf16[128,1024]{1,0:T(8,128)(2,1)S(1)}, bf16[128,1024]{1,0:T(8,128)(2,1)S(1)}, u32[]{:S(2)}, u32[]{:S(2)}) collective-permute-start(bf16[128,1024]{1,0:T(8,128)(2,1)S(1)} %convert_element_type.146), channel_id=1, source_target_pairs={{15,0},{0,1},{1,2},{2,3},{3,4},{4,5},{5,6},{6,7},{7,8},{8,9},{9,10... | collective-permute-start | bytes 786440 | tf_op jit(solution)/shard_map/while/body/eval_jaxpr/ppermute | solution.py:13
  399.8 38.4 %copy-start.13 = (bf16[128,512]{1,0:T(8,128)(2,1)S(1)}, bf16[128,512]{1,0:T(8,128)(2,1)}, u32[]{:S(2)}) copy-start(bf16[128,512]{1,0:T(8,128)(2,1)} %copy-done.12) | copy-start | bytes 393220
  399.8 38.4 %copy-start.23 = (f32[128]{0:T(128)S(1)}, f32[128]{0:T(128)}, u32[]{:S(2)}) copy-start(f32[128]{0:T(128)} %copy-done.22) | copy-start | bytes 1540
  399.8 38.4 %copy-start.25 = (f32[128]{0:T(128)S(1)}, f32[128]{0:T(128)}, u32[]{:S(2)}) copy-start(f32[128]{0:T(128)} %copy-done.24) | copy-start | bytes 1540
Sparse Core Ops, SparseCore 0:
  398.9 36.6 reduce-scatter.1
